TPU v7x, 32 devices: a whole 2x2x4 slice. The times are simulated.
32 devices in a mesh: tm: 4 (over z), space: 8 (over y, x, core).
Axes of the slice: x: 2, y: 2, z: 4, core: 2. Of those that a mesh axis runs over, the one named last changes fastest.
Arguments:
- forward_states: bfloat16 [16, 4, 32, 8, 128], P('tm', None, 'space'), may hold values from -3 to 3
- adjoint_source: float32 [16, 4, 32, 8, 128], P('tm', None, 'space'), may hold values from -6 to 6
- source_gain: float32 [4, 32, 8, 128], P(None, 'space'), may hold values from -4 to 0.3
- guess_pairs: float32 [4, 2, 4, 32, 8, 128], P('tm', None, None, 'space'), may hold values from -6 to 6
Outputs:
- corrected: float32 [4, 2, 4, 32, 8, 128], P('tm', None, None, 'space')
- gradient: float32 [4, 32, 8, 128], P(None, 'space')
All inputs are finite; a program needn't handle non-finite values.
Results may differ from a plain program's by a relative error of at most 0.0003.
Values sent between devices are 32-bit elements; how exact they have to be, the bound alone decides.
A program may use at most 64 MiB of HBM per device.

v0:
```python
import jax
import jax.numpy as jnp
from jax import lax
from jax.sharding import PartitionSpec as P

SWEEPS = 4


diffusion = (2.4, 1.2, 0.6, 4.0)
fibre_weight = 128.0
reaction = (
    (-14.4, 7.2, -4.8, 2.4),
    (4.8, -19.2, 7.2, -4.8),
    (-7.2, 2.4, -12.0, 7.2),
    (4.8, -7.2, 2.4, -38.4),
)
self_rates = (-14.4, -19.2, -12.0, -38.4)
masses = (1.0, 1.0, 1.0, 0.0)
fine_rate = 3.0
coarse_rate = 0.75
time_step = 0.5
operator_scale = 0.0078125
state_weight = 0.1
gain_weight = 0.25


def with_halo(cells, sides, width):
    for axis, dim in sides:
        count = lax.axis_size(axis)
        ends = count - 1
        head = lax.slice_in_dim(cells, 0, width, axis=dim)
        tail = lax.slice_in_dim(cells, cells.shape[dim] - width, cells.shape[dim], axis=dim)
        cells = jnp.concatenate(
            [
                lax.ppermute(tail, axis, [(i, (i + 1) % count) for i in range(ends)]),
                cells,
                lax.ppermute(head, axis, [((i + 1) % count, i) for i in range(ends)]),
            ],
            axis=dim,
        )
    return cells


def passed_along(value, axis, steps):
    count = lax.axis_size(axis)
    initial, last = (max(0, -steps), min(count, count - steps))
    return lax.ppermute(value, axis, [(source, source + steps) for source in range(initial, last)])


def column(values):
    return jnp.array(values, jnp.float32).reshape(4, 1, 1, 1)


def from_below(field, axis):
    extent = field.shape[axis]
    retained = lax.slice_in_dim(field, 0, extent - 1, axis=axis)
    widths = [(0, 0)] * field.ndim
    widths[axis] = (1, 0)
    return jnp.pad(retained, widths)


def from_above(field, axis):
    extent = field.shape[axis]
    retained = lax.slice_in_dim(field, 1, extent, axis=axis)
    widths = [(0, 0)] * field.ndim
    widths[axis] = (0, 1)
    return jnp.pad(retained, widths)


def neighbours(field):
    running = fibre_weight * (from_below(field, 1) + from_above(field, 1))
    running = running + from_below(field, 2) + from_above(field, 2)
    return running + from_below(field, 3) + from_above(field, 3)


def coupling(field):
    stacked_rows = []
    for target in range(4):
        running = jnp.zeros_like(field[0])
        for source in range(4):
            if source != target:
                running = running + reaction[source][target] * field[source]
        stacked_rows.append(running)
    return jnp.stack(stacked_rows)


def jacobi_sweep(field, right_side, diagonal):
    spread = column(diffusion) * neighbours(field) + coupling(field)
    return (right_side + operator_scale * spread) / diagonal


def make_diagonal(state, source_gain, rate):
    stencil_total = (2.0 * fibre_weight + 4.0) * column(diffusion)
    spatial = operator_scale * (stencil_total - column(self_rates))
    return (
        rate * column(masses) + spatial + state_weight * state * state - gain_weight * source_gain
    )


def inside_mask(thickness):
    start_cell = lax.axis_index("space") * thickness - SWEEPS
    cell_index = start_cell + jnp.arange(thickness + 2 * SWEEPS, dtype=jnp.int32)
    return ((cell_index >= 0) & (cell_index < thickness * lax.axis_size("space"))).reshape(
        1, -1, 1, 1
    )


def guarded(wide_diagonal, inside):
    return jnp.where(inside, wide_diagonal, 1.0)


def relax(wide_right, safe_diagonal, inside):
    thickness = wide_right.shape[1] - 2 * SWEEPS
    iterate = jnp.where(inside, wide_right / safe_diagonal, 0.0)
    for sweep_count in range(SWEEPS):
        iterate = jnp.where(inside, jacobi_sweep(iterate, wide_right, safe_diagonal), 0.0)
    return iterate[:, SWEEPS : SWEEPS + thickness]


def implicit_solve(right_side, diagonal_info):
    thickness = right_side.shape[1]
    inside = inside_mask(thickness)
    widened = with_halo(jnp.stack([right_side, diagonal_info]), (("space", 2),), SWEEPS)
    return relax(widened[0], guarded(widened[1], inside), inside)


def coarse_step(pair, diagonal_info):
    solved = implicit_solve(column(masses) * (pair[0] - 0.25 * pair[1]), diagonal_info)
    return jnp.stack([solved, 0.5 * (solved + pair[0])])


def on_device(forward_states, adjoint_source, source_gain, guess_pairs):
    states = forward_states.astype(jnp.float32)
    mass = column(masses)
    local_steps = forward_states.shape[0]
    fine_diagonals = [
        make_diagonal(states[offset], source_gain, fine_rate) for offset in range(local_steps)
    ]
    coarse_diagonal = make_diagonal(states[0], source_gain, coarse_rate)
    later = passed_along(guess_pairs[0], "tm", -1)
    ahead_one, ahead_two = (later[0], later[1])
    adjoints = [None] * local_steps
    for offset in range(local_steps - 1, -1, -1):
        right_side = adjoint_source[offset] + mass * (4.0 * ahead_one - ahead_two)
        current = implicit_solve(right_side, fine_diagonals[offset])
        adjoints[offset] = current
        ahead_two, ahead_one = (ahead_one, current)
    running = adjoints[0] * states[0]
    for offset in range(1, local_steps):
        running = running + adjoints[offset] * states[offset]
    gradient = lax.psum(time_step * running, "tm")
    relaxed = jnp.stack([adjoints[0], adjoints[1]])
    following = passed_along(relaxed, "tm", -1)
    offsets = relaxed - coarse_step(following, coarse_diagonal)
    tm_count = lax.axis_size("tm")

    def advance(step_index, carried):
        incoming = passed_along(carried, "tm", -1)
        return coarse_step(incoming, coarse_diagonal) + offsets

    corrected = lax.fori_loop(0, tm_count, advance, jnp.zeros_like(offsets))
    return (corrected[None], gradient)


def solution(mesh):
    placed = (
        P("tm", None, "space", None, None),
        P("tm", None, "space", None, None),
        P(None, "space", None, None),
        P("tm", None, None, "space", None, None),
    )
    return jax.shard_map(
        on_device,
        mesh=mesh,
        in_specs=placed,
        out_specs=(P("tm", None, None, "space", None, None), P(None, "space", None, None)),
        check_vma=False,
    )
```

profile of v0, /device:TPU:3, one launch (start us, length us, event | category | flops | bytes accessed | tf_op | source)
XLA Modules:
  0.0 184.9 jit_solution(17200818279672020096)
XLA Ops:
  9.8 4.1 %collective-permute-done.3 = f32[2,4,4,8,128]{4,3,2,1,0:T(8,128)S(1)} collective-permute-done((f32[2,4,4,8,128]{4,3,2,1,0:T(8,128)}, f32[2,4,4,8,128]{4,3,2,1,0:T(8,128)S(1)}, u32[]{:S(2)}, u32[]{:S(2)}) %collective-permute-start.3) | collective-permute-done | bytes 131104 | tf_op jit(solution)/shard_map/ppermute | solution.py:47
  13.9 4.6 %collective-permute-start.4 = (f32[2,4,4,8,128]{4,3,2,1,0:T(8,128)S(1)}, f32[2,4,4,8,128]{4,3,2,1,0:T(8,128)S(1)}, u32[]{:S(2)}, u32[]{:S(2)}) collective-permute-start(f32[2,4,4,8,128]{4,3,2,1,0:T(8,128)S(1)} %pad_maximum_fusion.14), channel_id=1, source_target_pairs={{0,1},{1,2},{2,3},{3,4},{4,5},{5,6},{6,7},{8,9},{9,10},{10,11},{11... | collective-permute-start | bytes 393224 | tf_op jit(solution)/shard_map/ppermute | solution.py:35
  20.5 5.2 %collective-permute-done.5 = f32[2,4,4,8,128]{4,3,2,1,0:T(8,128)S(1)} collective-permute-done((f32[2,4,4,8,128]{4,3,2,1,0:T(8,128)S(1)}, f32[2,4,4,8,128]{4,3,2,1,0:T(8,128)S(1)}, u32[]{:S(2)}, u32[]{:S(2)}) %collective-permute-start.5) | collective-permute-done | bytes 131104 | tf_op jit(solution)/shard_map/ppermute | solution.py:37
  30.1 2.4 %collective-permute-start.7 = (f32[2,4,4,8,128]{4,3,2,1,0:T(8,128)S(1)}, f32[2,4,4,8,128]{4,3,2,1,0:T(8,128)S(1)}, u32[]{:S(2)}, u32[]{:S(2)}) collective-permute-start(f32[2,4,4,8,128]{4,3,2,1,0:T(8,128)S(1)} %pad_maximum_fusion.15), channel_id=1, source_target_pairs={{1,0},{2,1},{3,2},{4,3},{5,4},{6,5},{7,6},{9,8},{10,9},{11,10},{12... | collective-permute-start | bytes 393224 | tf_op jit(solution)/shard_map/ppermute | solution.py:37
  32.6 4.8 %collective-permute-done.7 = f32[2,4,4,8,128]{4,3,2,1,0:T(8,128)S(1)} collective-permute-done((f32[2,4,4,8,128]{4,3,2,1,0:T(8,128)S(1)}, f32[2,4,4,8,128]{4,3,2,1,0:T(8,128)S(1)}, u32[]{:S(2)}, u32[]{:S(2)}) %collective-permute-start.7) | collective-permute-done | bytes 131104 | tf_op jit(solution)/shard_map/ppermute | solution.py:37
  43.6 4.8 %collective-permute-done.9 = f32[2,4,4,8,128]{4,3,2,1,0:T(8,128)S(1)} collective-permute-done((f32[2,4,4,8,128]{4,3,2,1,0:T(8,128)S(1)}, f32[2,4,4,8,128]{4,3,2,1,0:T(8,128)S(1)}, u32[]{:S(2)}, u32[]{:S(2)}) %collective-permute-start.9) | collective-permute-done | bytes 131104 | tf_op jit(solution)/shard_map/ppermute | solution.py:37
  54.6 4.8 %collective-permute-done.11 = f32[2,4,4,8,128]{4,3,2,1,0:T(8,128)S(1)} collective-permute-done((f32[2,4,4,8,128]{4,3,2,1,0:T(8,128)S(1)}, f32[2,4,4,8,128]{4,3,2,1,0:T(8,128)S(1)}, u32[]{:S(2)}, u32[]{:S(2)}) %collective-permute-start.11) | collective-permute-done | bytes 131104 | tf_op jit(solution)/shard_map/ppermute | solution.py:37
  63.2 4.4 %collective-permute-done.12 = f32[2,4,4,8,128]{4,3,2,1,0:T(8,128)S(1)} collective-permute-done((f32[2,4,4,8,128]{4,3,2,1,0:T(8,128)S(1)}, f32[2,4,4,8,128]{4,3,2,1,0:T(8,128)S(1)}, u32[]{:S(2)}, u32[]{:S(2)}) %collective-permute-start.12) | collective-permute-done | bytes 131104 | tf_op jit(solution)/shard_map/ppermute | solution.py:47
  67.7 2.9 %collective-permute-start.13 = (f32[2,4,4,8,128]{4,3,2,1,0:T(8,128)S(1)}, f32[2,4,4,8,128]{4,3,2,1,0:T(8,128)S(1)}, u32[]{:S(2)}, u32[]{:S(2)}) collective-permute-start(f32[2,4,4,8,128]{4,3,2,1,0:T(8,128)S(1)} %pad_maximum_fusion.19), channel_id=1, source_target_pairs={{0,1},{1,2},{2,3},{3,4},{4,5},{5,6},{6,7},{8,9},{9,10},{10,11},{11... | collective-permute-start | bytes 393224 | tf_op jit(solution)/shard_map/ppermute | solution.py:35
  72.6 5.2 %collective-permute-done.14 = f32[2,4,4,8,128]{4,3,2,1,0:T(8,128)S(1)} collective-permute-done((f32[2,4,4,8,128]{4,3,2,1,0:T(8,128)S(1)}, f32[2,4,4,8,128]{4,3,2,1,0:T(8,128)S(1)}, u32[]{:S(2)}, u32[]{:S(2)}) %collective-permute-start.14) | collective-permute-done | bytes 131104 | tf_op jit(solution)/shard_map/ppermute | solution.py:37
  79.7 25.2 %all-reduce.146.cloned.1.call-done = f32[4,4,8,128]{3,2,1,0:T(8,128)} async-done(((f32[4,4,8,128]{3,2,1,0:T(8,128)}), f32[4,4,8,128]{3,2,1,0:T(8,128)}) %all-reduce.146.cloned.1.call-update) | async-done | bytes 65552 | tf_op jit(solution)/shard_map/psum | solution.py:151
  104.9 72.4 %while.15 = (s32[]{:T(128)}, f32[2,4,4,8,128]{4,3,2,1,0:T(8,128)S(1)}, f32[4,4,8,128]{3,2,1,0:T(8,128)S(1)}, f32[2,4,4,8,128]{4,3,2,1,0:T(8,128)S(1)}, s32[]{:T(...) while((s32[]{:T(128)}, ...), condition=%wide.region_1.2_spmd.clone.clone.clone, body=%wide.region_0.1_spmd.sunk.clone.clone.clone.sunk | while | flops 4505655 | bytes 22770104 | solution.py:161
  106.4 4.4 %collective-permute-done = f32[2,4,4,8,128]{4,3,2,1,0:T(8,128)S(1)} collective-permute-done((f32[2,4,4,8,128]{4,3,2,1,0:T(8,128)S(1)}, f32[2,4,4,8,128]{4,3,2,1,0:T(8,128)S(1)}, u32[]{:S(2)}, u32[]{:S(2)}) %collective-permute-start) | collective-permute-done | bytes 131104 | tf_op jit(solution)/shard_map/while/body/eval_jaxpr/ppermute | solution.py:47
  110.9 5.7 %collective-permute-start.1 = (f32[2,4,4,8,128]{4,3,2,1,0:T(8,128)S(1)}, f32[2,4,4,8,128]{4,3,2,1,0:T(8,128)S(1)}, u32[]{:S(2)}, u32[]{:S(2)}) collective-permute-start(f32[2,4,4,8,128]{4,3,2,1,0:T(8,128)S(1)} %pad_maximum_fusion.28), channel_id=1, source_target_pairs={{1,0},{2,1},{3,2},{4,3},{5,4},{6,5},{7,6},{9,8},{10,9},{11,10},{12... | collective-permute-start | bytes 393224 | tf_op jit(solution)/shard_map/while/body/eval_jaxpr/ppermute | solution.py:37
  116.6 3.0 %collective-permute-start.2 = (f32[2,4,4,8,128]{4,3,2,1,0:T(8,128)S(1)}, f32[2,4,4,8,128]{4,3,2,1,0:T(8,128)S(1)}, u32[]{:S(2)}, u32[]{:S(2)}) collective-permute-start(f32[2,4,4,8,128]{4,3,2,1,0:T(8,128)S(1)} %pad_maximum_fusion.28), channel_id=1, source_target_pairs={{0,1},{1,2},{2,3},{3,4},{4,5},{5,6},{6,7},{8,9},{9,10},{10,11},{11... | collective-permute-start | bytes 393224 | tf_op jit(solution)/shard_map/while/body/eval_jaxpr/ppermute | solution.py:35
  124.7 4.4 %collective-permute-done = f32[2,4,4,8,128]{4,3,2,1,0:T(8,128)S(1)} collective-permute-done((f32[2,4,4,8,128]{4,3,2,1,0:T(8,128)S(1)}, f32[2,4,4,8,128]{4,3,2,1,0:T(8,128)S(1)}, u32[]{:S(2)}, u32[]{:S(2)}) %collective-permute-start) | collective-permute-done | bytes 131104 | tf_op jit(solution)/shard_map/while/body/eval_jaxpr/ppermute | solution.py:47
  129.2 4.4 %collective-permute-start.1 = (f32[2,4,4,8,128]{4,3,2,1,0:T(8,128)S(1)}, f32[2,4,4,8,128]{4,3,2,1,0:T(8,128)S(1)}, u32[]{:S(2)}, u32[]{:S(2)}) collective-permute-start(f32[2,4,4,8,128]{4,3,2,1,0:T(8,128)S(1)} %pad_maximum_fusion.28), channel_id=1, source_target_pairs={{1,0},{2,1},{3,2},{4,3},{5,4},{6,5},{7,6},{9,8},{10,9},{11,10},{12... | collective-permute-start | bytes 393224 | tf_op jit(solution)/shard_map/while/body/eval_jaxpr/ppermute | solution.py:37
  133.7 3.9 %collective-permute-start.2 = (f32[2,4,4,8,128]{4,3,2,1,0:T(8,128)S(1)}, f32[2,4,4,8,128]{4,3,2,1,0:T(8,128)S(1)}, u32[]{:S(2)}, u32[]{:S(2)}) collective-permute-start(f32[2,4,4,8,128]{4,3,2,1,0:T(8,128)S(1)} %pad_maximum_fusion.28), channel_id=1, source_target_pairs={{0,1},{1,2},{2,3},{3,4},{4,5},{5,6},{6,7},{8,9},{9,10},{10,11},{11... | collective-permute-start | bytes 393224 | tf_op jit(solution)/shard_map/while/body/eval_jaxpr/ppermute | solution.py:35
  142.7 5.2 %collective-permute-done = f32[2,4,4,8,128]{4,3,2,1,0:T(8,128)S(1)} collective-permute-done((f32[2,4,4,8,128]{4,3,2,1,0:T(8,128)S(1)}, f32[2,4,4,8,128]{4,3,2,1,0:T(8,128)S(1)}, u32[]{:S(2)}, u32[]{:S(2)}) %collective-permute-start) | collective-permute-done | bytes 131104 | tf_op jit(solution)/shard_map/while/body/eval_jaxpr/ppermute | solution.py:47
  148.0 3.2 %collective-permute-start.1 = (f32[2,4,4,8,128]{4,3,2,1,0:T(8,128)S(1)}, f32[2,4,4,8,128]{4,3,2,1,0:T(8,128)S(1)}, u32[]{:S(2)}, u32[]{:S(2)}) collective-permute-start(f32[2,4,4,8,128]{4,3,2,1,0:T(8,128)S(1)} %pad_maximum_fusion.28), channel_id=1, source_target_pairs={{1,0},{2,1},{3,2},{4,3},{5,4},{6,5},{7,6},{9,8},{10,9},{11,10},{12... | collective-permute-start | bytes 393224 | tf_op jit(solution)/shard_map/while/body/eval_jaxpr/ppermute | solution.py:37
  151.2 4.3 %collective-permute-start.2 = (f32[2,4,4,8,128]{4,3,2,1,0:T(8,128)S(1)}, f32[2,4,4,8,128]{4,3,2,1,0:T(8,128)S(1)}, u32[]{:S(2)}, u32[]{:S(2)}) collective-permute-start(f32[2,4,4,8,128]{4,3,2,1,0:T(8,128)S(1)} %pad_maximum_fusion.28), channel_id=1, source_target_pairs={{0,1},{1,2},{2,3},{3,4},{4,5},{5,6},{6,7},{8,9},{9,10},{10,11},{11... | collective-permute-start | bytes 393224 | tf_op jit(solution)/shard_map/while/body/eval_jaxpr/ppermute | solution.py:35
  160.7 5.7 %collective-permute-done = f32[2,4,4,8,128]{4,3,2,1,0:T(8,128)S(1)} collective-permute-done((f32[2,4,4,8,128]{4,3,2,1,0:T(8,128)S(1)}, f32[2,4,4,8,128]{4,3,2,1,0:T(8,128)S(1)}, u32[]{:S(2)}, u32[]{:S(2)}) %collective-permute-start) | collective-permute-done | bytes 131104 | tf_op jit(solution)/shard_map/while/body/eval_jaxpr/ppermute | solution.py:47
  166.5 2.7 %collective-permute-start.1 = (f32[2,4,4,8,128]{4,3,2,1,0:T(8,128)S(1)}, f32[2,4,4,8,128]{4,3,2,1,0:T(8,128)S(1)}, u32[]{:S(2)}, u32[]{:S(2)}) collective-permute-start(f32[2,4,4,8,128]{4,3,2,1,0:T(8,128)S(1)} %pad_maximum_fusion.28), channel_id=1, source_target_pairs={{1,0},{2,1},{3,2},{4,3},{5,4},{6,5},{7,6},{9,8},{10,9},{11,10},{12... | collective-permute-start | bytes 393224 | tf_op jit(solution)/shard_map/while/body/eval_jaxpr/ppermute | solution.py:37
  169.2 4.3 %collective-permute-start.2 = (f32[2,4,4,8,128]{4,3,2,1,0:T(8,128)S(1)}, f32[2,4,4,8,128]{4,3,2,1,0:T(8,128)S(1)}, u32[]{:S(2)}, u32[]{:S(2)}) collective-permute-start(f32[2,4,4,8,128]{4,3,2,1,0:T(8,128)S(1)} %pad_maximum_fusion.28), channel_id=1, source_target_pairs={{0,1},{1,2},{2,3},{3,4},{4,5},{5,6},{6,7},{8,9},{9,10},{10,11},{11... | collective-permute-start | bytes 393224 | tf_op jit(solution)/shard_map/while/body/eval_jaxpr/ppermute | solution.py:35
  (303 shorter events, 49.2 us)
Async XLA Ops:
  7.2 97.8 %all-reduce.146.cloned.1.call-start = ((), (), s32[]{:S(2)}) async-start(), calls=%async_computation | async-start | bytes 131072 | tf_op jit(solution)/shard_map/psum | solution.py:151
  7.2 6.6 %collective-permute-start.3 = (f32[2,4,4,8,128]{4,3,2,1,0:T(8,128)}, f32[2,4,4,8,128]{4,3,2,1,0:T(8,128)S(1)}, u32[]{:S(2)}, u32[]{:S(2)}) collective-permute-start(f32[2,4,4,8,128]{4,3,2,1,0:T(8,128)} %bitcast.253), channel_id=1, source_target_pairs={{8,0},{16,8},{24,16},{9,1},{17,9},{25,17},{10,2},{18,10},{26,18},{... | collective-permute-start | bytes 393224 | tf_op jit(solution)/shard_map/ppermute | solution.py:47
  13.9 6.6 %collective-permute-start.4 = (f32[2,4,4,8,128]{4,3,2,1,0:T(8,128)S(1)}, f32[2,4,4,8,128]{4,3,2,1,0:T(8,128)S(1)}, u32[]{:S(2)}, u32[]{:S(2)}) collective-permute-start(f32[2,4,4,8,128]{4,3,2,1,0:T(8,128)S(1)} %pad_maximum_fusion.14), channel_id=1, source_target_pairs={{0,1},{1,2},{2,3},{3,4},{4,5},{5,6},{6,7},{8,9},{9,10},{10,11},{11... | collective-permute-start | bytes 393224 | tf_op jit(solution)/shard_map/ppermute | solution.py:35
  18.5 7.2 %collective-permute-start.5 = (f32[2,4,4,8,128]{4,3,2,1,0:T(8,128)S(1)}, f32[2,4,4,8,128]{4,3,2,1,0:T(8,128)S(1)}, u32[]{:S(2)}, u32[]{:S(2)}) collective-permute-start(f32[2,4,4,8,128]{4,3,2,1,0:T(8,128)S(1)} %pad_maximum_fusion.14), channel_id=1, source_target_pairs={{1,0},{2,1},{3,2},{4,3},{5,4},{6,5},{7,6},{9,8},{10,9},{11,10},{12... | collective-permute-start | bytes 393224 | tf_op jit(solution)/shard_map/ppermute | solution.py:37
  28.2 4.3 %collective-permute-start.6 = (f32[2,4,4,8,128]{4,3,2,1,0:T(8,128)S(1)}, f32[2,4,4,8,128]{4,3,2,1,0:T(8,128)S(1)}, u32[]{:S(2)}, u32[]{:S(2)}) collective-permute-start(f32[2,4,4,8,128]{4,3,2,1,0:T(8,128)S(1)} %pad_maximum_fusion.15), channel_id=1, source_target_pairs={{0,1},{1,2},{2,3},{3,4},{4,5},{5,6},{6,7},{8,9},{9,10},{10,11},{11... | collective-permute-start | bytes 393224 | tf_op jit(solution)/shard_map/ppermute | solution.py:35
  30.1 7.2 %collective-permute-start.7 = (f32[2,4,4,8,128]{4,3,2,1,0:T(8,128)S(1)}, f32[2,4,4,8,128]{4,3,2,1,0:T(8,128)S(1)}, u32[]{:S(2)}, u32[]{:S(2)}) collective-permute-start(f32[2,4,4,8,128]{4,3,2,1,0:T(8,128)S(1)} %pad_maximum_fusion.15), channel_id=1, source_target_pairs={{1,0},{2,1},{3,2},{4,3},{5,4},{6,5},{7,6},{9,8},{10,9},{11,10},{12... | collective-permute-start | bytes 393224 | tf_op jit(solution)/shard_map/ppermute | solution.py:37
  39.2 4.3 %collective-permute-start.8 = (f32[2,4,4,8,128]{4,3,2,1,0:T(8,128)S(1)}, f32[2,4,4,8,128]{4,3,2,1,0:T(8,128)S(1)}, u32[]{:S(2)}, u32[]{:S(2)}) collective-permute-start(f32[2,4,4,8,128]{4,3,2,1,0:T(8,128)S(1)} %pad_maximum_fusion.16), channel_id=1, source_target_pairs={{0,1},{1,2},{2,3},{3,4},{4,5},{5,6},{6,7},{8,9},{9,10},{10,11},{11... | collective-permute-start | bytes 393224 | tf_op jit(solution)/shard_map/ppermute | solution.py:35
  41.2 7.2 %collective-permute-start.9 = (f32[2,4,4,8,128]{4,3,2,1,0:T(8,128)S(1)}, f32[2,4,4,8,128]{4,3,2,1,0:T(8,128)S(1)}, u32[]{:S(2)}, u32[]{:S(2)}) collective-permute-start(f32[2,4,4,8,128]{4,3,2,1,0:T(8,128)S(1)} %pad_maximum_fusion.16), channel_id=1, source_target_pairs={{1,0},{2,1},{3,2},{4,3},{5,4},{6,5},{7,6},{9,8},{10,9},{11,10},{12... | collective-permute-start | bytes 393224 | tf_op jit(solution)/shard_map/ppermute | solution.py:37
  52.2 7.2 %collective-permute-start.11 = (f32[2,4,4,8,128]{4,3,2,1,0:T(8,128)S(1)}, f32[2,4,4,8,128]{4,3,2,1,0:T(8,128)S(1)}, u32[]{:S(2)}, u32[]{:S(2)}) collective-permute-start(f32[2,4,4,8,128]{4,3,2,1,0:T(8,128)S(1)} %pad_maximum_fusion.17), channel_id=1, source_target_pairs={{1,0},{2,1},{3,2},{4,3},{5,4},{6,5},{7,6},{9,8},{10,9},{11,10},{12... | collective-permute-start | bytes 393224 | tf_op jit(solution)/shard_map/ppermute | solution.py:37
  61.9 5.7 %collective-permute-start.12 = (f32[2,4,4,8,128]{4,3,2,1,0:T(8,128)S(1)}, f32[2,4,4,8,128]{4,3,2,1,0:T(8,128)S(1)}, u32[]{:S(2)}, u32[]{:S(2)}) collective-permute-start(f32[2,4,4,8,128]{4,3,2,1,0:T(8,128)S(1)} %pad_maximum_fusion.18), channel_id=1, source_target_pairs={{8,0},{16,8},{24,16},{9,1},{17,9},{25,17},{10,2},{18,10},{26,18},{... | collective-permute-start | bytes 393224 | tf_op jit(solution)/shard_map/ppermute | solution.py:47
  67.7 4.9 %collective-permute-start.13 = (f32[2,4,4,8,128]{4,3,2,1,0:T(8,128)S(1)}, f32[2,4,4,8,128]{4,3,2,1,0:T(8,128)S(1)}, u32[]{:S(2)}, u32[]{:S(2)}) collective-permute-start(f32[2,4,4,8,128]{4,3,2,1,0:T(8,128)S(1)} %pad_maximum_fusion.19), channel_id=1, source_target_pairs={{0,1},{1,2},{2,3},{3,4},{4,5},{5,6},{6,7},{8,9},{9,10},{10,11},{11... | collective-permute-start | bytes 393224 | tf_op jit(solution)/shard_map/ppermute | solution.py:35
  70.6 7.2 %collective-permute-start.14 = (f32[2,4,4,8,128]{4,3,2,1,0:T(8,128)S(1)}, f32[2,4,4,8,128]{4,3,2,1,0:T(8,128)S(1)}, u32[]{:S(2)}, u32[]{:S(2)}) collective-permute-start(f32[2,4,4,8,128]{4,3,2,1,0:T(8,128)S(1)} %pad_maximum_fusion.19), channel_id=1, source_target_pairs={{1,0},{2,1},{3,2},{4,3},{5,4},{6,5},{7,6},{9,8},{10,9},{11,10},{12... | collective-permute-start | bytes 393224 | tf_op jit(solution)/shard_map/ppermute | solution.py:37
  105.0 5.8 %collective-permute-start = (f32[2,4,4,8,128]{4,3,2,1,0:T(8,128)S(1)}, f32[2,4,4,8,128]{4,3,2,1,0:T(8,128)S(1)}, u32[]{:S(2)}, u32[]{:S(2)}) collective-permute-start(f32[2,4,4,8,128]{4,3,2,1,0:T(8,128)S(1)} %broadcast_select_fusion.2), channel_id=1, source_target_pairs={{8,0},{16,8},{24,16},{9,1},{17,9},{25,17},{10,2},{18,10},{26,18},{... | collective-permute-start | bytes 393224 | tf_op jit(solution)/shard_map/while/body/eval_jaxpr/ppermute | solution.py:47
  110.9 9.4 %collective-permute-start.1 = (f32[2,4,4,8,128]{4,3,2,1,0:T(8,128)S(1)}, f32[2,4,4,8,128]{4,3,2,1,0:T(8,128)S(1)}, u32[]{:S(2)}, u32[]{:S(2)}) collective-permute-start(f32[2,4,4,8,128]{4,3,2,1,0:T(8,128)S(1)} %pad_maximum_fusion.28), channel_id=1, source_target_pairs={{1,0},{2,1},{3,2},{4,3},{5,4},{6,5},{7,6},{9,8},{10,9},{11,10},{12... | collective-permute-start | bytes 393224 | tf_op jit(solution)/shard_map/while/body/eval_jaxpr/ppermute | solution.py:37
  116.6 4.9 %collective-permute-start.2 = (f32[2,4,4,8,128]{4,3,2,1,0:T(8,128)S(1)}, f32[2,4,4,8,128]{4,3,2,1,0:T(8,128)S(1)}, u32[]{:S(2)}, u32[]{:S(2)}) collective-permute-start(f32[2,4,4,8,128]{4,3,2,1,0:T(8,128)S(1)} %pad_maximum_fusion.28), channel_id=1, source_target_pairs={{0,1},{1,2},{2,3},{3,4},{4,5},{5,6},{6,7},{8,9},{9,10},{10,11},{11... | collective-permute-start | bytes 393224 | tf_op jit(solution)/shard_map/while/body/eval_jaxpr/ppermute | solution.py:35
  123.4 5.7 %collective-permute-start = (f32[2,4,4,8,128]{4,3,2,1,0:T(8,128)S(1)}, f32[2,4,4,8,128]{4,3,2,1,0:T(8,128)S(1)}, u32[]{:S(2)}, u32[]{:S(2)}) collective-permute-start(f32[2,4,4,8,128]{4,3,2,1,0:T(8,128)S(1)} %broadcast_select_fusion.2), channel_id=1, source_target_pairs={{8,0},{16,8},{24,16},{9,1},{17,9},{25,17},{10,2},{18,10},{26,18},{... | collective-permute-start | bytes 393224 | tf_op jit(solution)/shard_map/while/body/eval_jaxpr/ppermute | solution.py:47
  129.2 9.0 %collective-permute-start.1 = (f32[2,4,4,8,128]{4,3,2,1,0:T(8,128)S(1)}, f32[2,4,4,8,128]{4,3,2,1,0:T(8,128)S(1)}, u32[]{:S(2)}, u32[]{:S(2)}) collective-permute-start(f32[2,4,4,8,128]{4,3,2,1,0:T(8,128)S(1)} %pad_maximum_fusion.28), channel_id=1, source_target_pairs={{1,0},{2,1},{3,2},{4,3},{5,4},{6,5},{7,6},{9,8},{10,9},{11,10},{12... | collective-permute-start | bytes 393224 | tf_op jit(solution)/shard_map/while/body/eval_jaxpr/ppermute | solution.py:37
  133.7 5.8 %collective-permute-start.2 = (f32[2,4,4,8,128]{4,3,2,1,0:T(8,128)S(1)}, f32[2,4,4,8,128]{4,3,2,1,0:T(8,128)S(1)}, u32[]{:S(2)}, u32[]{:S(2)}) collective-permute-start(f32[2,4,4,8,128]{4,3,2,1,0:T(8,128)S(1)} %pad_maximum_fusion.28), channel_id=1, source_target_pairs={{0,1},{1,2},{2,3},{3,4},{4,5},{5,6},{6,7},{8,9},{9,10},{10,11},{11... | collective-permute-start | bytes 393224 | tf_op jit(solution)/shard_map/while/body/eval_jaxpr/ppermute | solution.py:35
  141.4 6.5 %collective-permute-start = (f32[2,4,4,8,128]{4,3,2,1,0:T(8,128)S(1)}, f32[2,4,4,8,128]{4,3,2,1,0:T(8,128)S(1)}, u32[]{:S(2)}, u32[]{:S(2)}) collective-permute-start(f32[2,4,4,8,128]{4,3,2,1,0:T(8,128)S(1)} %broadcast_select_fusion.2), channel_id=1, source_target_pairs={{8,0},{16,8},{24,16},{9,1},{17,9},{25,17},{10,2},{18,10},{26,18},{... | collective-permute-start | bytes 393224 | tf_op jit(solution)/shard_map/while/body/eval_jaxpr/ppermute | solution.py:47
  148.0 8.3 %collective-permute-start.1 = (f32[2,4,4,8,128]{4,3,2,1,0:T(8,128)S(1)}, f32[2,4,4,8,128]{4,3,2,1,0:T(8,128)S(1)}, u32[]{:S(2)}, u32[]{:S(2)}) collective-permute-start(f32[2,4,4,8,128]{4,3,2,1,0:T(8,128)S(1)} %pad_maximum_fusion.28), channel_id=1, source_target_pairs={{1,0},{2,1},{3,2},{4,3},{5,4},{6,5},{7,6},{9,8},{10,9},{11,10},{12... | collective-permute-start | bytes 393224 | tf_op jit(solution)/shard_map/while/body/eval_jaxpr/ppermute | solution.py:37
  151.2 6.3 %collective-permute-start.2 = (f32[2,4,4,8,128]{4,3,2,1,0:T(8,128)S(1)}, f32[2,4,4,8,128]{4,3,2,1,0:T(8,128)S(1)}, u32[]{:S(2)}, u32[]{:S(2)}) collective-permute-start(f32[2,4,4,8,128]{4,3,2,1,0:T(8,128)S(1)} %pad_maximum_fusion.28), channel_id=1, source_target_pairs={{0,1},{1,2},{2,3},{3,4},{4,5},{5,6},{6,7},{8,9},{9,10},{10,11},{11... | collective-permute-start | bytes 393224 | tf_op jit(solution)/shard_map/while/body/eval_jaxpr/ppermute | solution.py:35
  159.4 7.0 %collective-permute-start = (f32[2,4,4,8,128]{4,3,2,1,0:T(8,128)S(1)}, f32[2,4,4,8,128]{4,3,2,1,0:T(8,128)S(1)}, u32[]{:S(2)}, u32[]{:S(2)}) collective-permute-start(f32[2,4,4,8,128]{4,3,2,1,0:T(8,128)S(1)} %broadcast_select_fusion.2), channel_id=1, source_target_pairs={{8,0},{16,8},{24,16},{9,1},{17,9},{25,17},{10,2},{18,10},{26,18},{... | collective-permute-start | bytes 393224 | tf_op jit(solution)/shard_map/while/body/eval_jaxpr/ppermute | solution.py:47
  166.5 7.8 %collective-permute-start.1 = (f32[2,4,4,8,128]{4,3,2,1,0:T(8,128)S(1)}, f32[2,4,4,8,128]{4,3,2,1,0:T(8,128)S(1)}, u32[]{:S(2)}, u32[]{:S(2)}) collective-permute-start(f32[2,4,4,8,128]{4,3,2,1,0:T(8,128)S(1)} %pad_maximum_fusion.28), channel_id=1, source_target_pairs={{1,0},{2,1},{3,2},{4,3},{5,4},{6,5},{7,6},{9,8},{10,9},{11,10},{12... | collective-permute-start | bytes 393224 | tf_op jit(solution)/shard_map/while/body/eval_jaxpr/ppermute | solution.py:37
  169.2 6.3 %collective-permute-start.2 = (f32[2,4,4,8,128]{4,3,2,1,0:T(8,128)S(1)}, f32[2,4,4,8,128]{4,3,2,1,0:T(8,128)S(1)}, u32[]{:S(2)}, u32[]{:S(2)}) collective-permute-start(f32[2,4,4,8,128]{4,3,2,1,0:T(8,128)S(1)} %pad_maximum_fusion.28), channel_id=1, source_target_pairs={{0,1},{1,2},{2,3},{3,4},{4,5},{5,6},{6,7},{8,9},{9,10},{10,11},{11... | collective-permute-start | bytes 393224 | tf_op jit(solution)/shard_map/while/body/eval_jaxpr/ppermute | solution.py:35
  (9 other events, 93.7 us)
Sparse Core Ops, SparseCore 0:
  72.7 32.1 all-reduce.145
where the time goes:
time: 187 us; the launch traced here: 185 us
  waiting for transfers between devices  85.4 us (46%)
  starting transfers between devices  64 us (34%)
  between operations  15.2 us (8%)
  other arithmetic  11.6 us (6%)
  local copies, waits for them, and re-layouts  7.76 us (4%)
    ppermute x9, starting transfers between devices, with_halo(): lax.ppermute(tail, axis, [(i, (i + 1) % count) for i in range(ends)])  28.8 us
    ppermute x6, waiting for transfers between devices, passed_along(): lax.ppermute(value, axis, [(source, source + steps) for source in range(i...  28.2 us
    ppermute x9, starting transfers between devices, with_halo(): lax.ppermute(head, axis, [((i + 1) % count, i) for i in range(ends)])  27.2 us
    ppermute x9, waiting for transfers between devices, with_halo(): lax.ppermute(head, axis, [((i + 1) % count, i) for i in range(ends)])  27.1 us
    psum x1, waiting for transfers between devices, on_device(): gradient = lax.psum(time_step * running, 'tm')  25.2 us
    ppermute x6, starting transfers between devices, passed_along(): lax.ppermute(value, axis, [(source, source + steps) for source in range(i...  8.02 us
    slice x108, local copies, waits for them, and re-layouts, from_below(): retained = lax.slice_in_dim(field, 0, extent - 1, axis=axis)  5.91 us
    ppermute x9, waiting for transfers between devices, with_halo(): lax.ppermute(tail, axis, [(i, (i + 1) % count) for i in range(ends)])  4.88 us
  transfers between devices with their start and end apart: 25, of which 20 were waited for; matrix products, arithmetic and copies ran while one was open for 2% of the time, Pallas kernels for 0%

commit v1 on v0

v1 whole, which is shorter than its diff:
```python
import functools

import jax
import jax.numpy as jnp
from jax import lax
from jax.experimental import pallas as pl
from jax.experimental.pallas import tpu as pltpu
from jax.sharding import PartitionSpec as P

SWEEPS = 4
FIELDS = 4
MASSIVE = 3

diffusion = (2.4, 1.2, 0.6, 4.0)
fibre_weight = 128.0
reaction = (
    (-14.4, 7.2, -4.8, 2.4),
    (4.8, -19.2, 7.2, -4.8),
    (-7.2, 2.4, -12.0, 7.2),
    (4.8, -7.2, 2.4, -38.4),
)
self_rates = (-14.4, -19.2, -12.0, -38.4)
masses = (1.0, 1.0, 1.0, 0.0)
fine_rate = 3.0
coarse_rate = 0.75
time_step = 0.5
operator_scale = 0.0078125
state_weight = 0.1
gain_weight = 0.25

MESH = pl.DeviceIdType.MESH


def kernel(
    steps, thick, tms, spaces,
    states_ref, source_ref, gain_ref, guess_ref,
    corrected_ref, gradient_ref,
    inv, right, rel_right, cor_right, xa, xb, adj, zero_q, rel_q, cor_q, offs, cor,
    w_src, w_got, g_src, g_got, rel_src, rel_p0, cor_src, cor_p0,
    part, part_got, whole,
    halo_send, halo_recv, z_send, z_recv, grad_send, grad_recv,
):
    t = lax.axis_index("tm")
    s = lax.axis_index("space")
    has_up, has_dn = s < spaces - 1, s > 0
    has_next, has_prev = t < tms - 1, t > 0
    wide = thick + 2 * SWEEPS
    own = pl.ds(SWEEPS, thick)
    low = pl.ds(0, SWEEPS)
    high = pl.ds(SWEEPS + thick, SWEEPS)
    coarse = steps
    row = lax.broadcasted_iota(jnp.int32, (8, 128), 0)
    col = lax.broadcasted_iota(jnp.int32, (8, 128), 1)

    def halo_copies(index, view):
        up = pltpu.make_async_remote_copy(
            view(own), view(low), halo_send.at[index, 0], halo_recv.at[index, 0],
            device_id={"space": s + 1}, device_id_type=MESH,
        )
        dn = pltpu.make_async_remote_copy(
            view(own), view(high), halo_send.at[index, 1], halo_recv.at[index, 1],
            device_id={"space": s - 1}, device_id_type=MESH,
        )
        return up, dn

    def halo_start(copies):
        pl.when(has_up)(copies[0].start)
        pl.when(has_dn)(copies[1].start)

    def halo_wait(copies):
        pl.when(has_dn)(copies[0].wait_recv)
        pl.when(has_up)(copies[1].wait_recv)

    def halo_sent(copies):
        pl.when(has_up)(copies[0].wait_send)
        pl.when(has_dn)(copies[1].wait_send)

    def to_previous(index, src, dst):
        return pltpu.make_async_remote_copy(
            src, dst, z_send.at[index], z_recv.at[index],
            device_id={"tm": t - 1}, device_id_type=MESH,
        )

    inv_copies = [
        halo_copies(n, lambda p, n=n: inv.at[n, :, p]) for n in range(steps + 1)
    ]
    last = steps - 1
    right_copies = [
        halo_copies(
            steps + 1 + n,
            (lambda p, n=n: right.at[n, :, p])
            if n == last
            else (lambda p, n=n: right.at[n, pl.ds(0, MASSIVE), p]),
        )
        for n in range(steps)
    ]
    rest_copies = halo_copies(
        2 * steps + 1, lambda p: right.at[pl.ds(0, last), MASSIVE, p]
    )
    rel_copies = halo_copies(
        2 * steps + 2, lambda p: rel_right.at[pl.ds(0, MASSIVE), p]
    )
    cor_copies = halo_copies(
        2 * steps + 3, lambda p: cor_right.at[pl.ds(0, MASSIVE), p]
    )
    z_w = to_previous(0, w_src, w_got)
    z_g = to_previous(1, g_src, g_got)
    z_rel = to_previous(2, rel_src, rel_right.at[pl.ds(0, MASSIVE), own])
    z_rel_p0 = to_previous(3, adj.at[0], rel_p0)
    z_cor = to_previous(4, cor_src, cor_right.at[pl.ds(0, MASSIVE), own])
    z_cor_p0 = to_previous(5, cor.at[0], cor_p0)

    rel_right[...] = jnp.zeros_like(rel_right)
    cor_right[...] = jnp.zeros_like(cor_right)

    def clear(span):
        inv[:, :, span] = jnp.zeros((steps + 1, FIELDS, SWEEPS, 8, 128), jnp.float32)
        right[:, :, span] = jnp.zeros((steps, FIELDS, SWEEPS, 8, 128), jnp.float32)

    @pl.when(s == 0)
    def _():
        clear(low)

    @pl.when(s == spaces - 1)
    def _():
        clear(high)

    @pl.when(t == tms - 1)
    def _():
        w_got[...] = jnp.zeros_like(w_got)
        g_got[...] = jnp.zeros_like(g_got)

    barrier = pltpu.get_barrier_semaphore()
    for hop in range(1, tms):
        pl.semaphore_signal(
            barrier, inc=1, device_id={"tm": lax.rem(t + hop, tms)}, device_id_type=MESH
        )

    @pl.when(has_up)
    def _():
        pl.semaphore_signal(barrier, inc=1, device_id={"space": s + 1}, device_id_type=MESH)

    @pl.when(has_dn)
    def _():
        pl.semaphore_signal(barrier, inc=1, device_id={"space": s - 1}, device_id_type=MESH)

    def fill_inverse(slot, n, rate):
        for i in range(FIELDS):
            u = states_ref[n, i].astype(jnp.float32)
            base = rate * masses[i] + operator_scale * (
                (2.0 * fibre_weight + 4.0) * diffusion[i] - self_rates[i]
            )
            diagonal = base + state_weight * u * u - gain_weight * gain_ref[i]
            inv[slot, i, own] = 1.0 / diagonal

    for i in range(MASSIVE):
        w_src[i] = 4.0 * guess_ref[0, 0, i] - guess_ref[0, 1, i]
        g_src[i] = guess_ref[0, 0, i]
    fill_inverse(last, last, fine_rate)

    pl.semaphore_wait(
        barrier, tms - 1 + has_up.astype(jnp.int32) + has_dn.astype(jnp.int32)
    )

    @pl.when(has_prev)
    def _():
        z_w.start()
        z_g.start()

    halo_start(inv_copies[last])
    for n in range(last):
        fill_inverse(n, n, fine_rate)
    fill_inverse(coarse, 0, coarse_rate)
    for n in range(steps):
        right[n, MASSIVE, own] = source_ref[n, MASSIVE]
    pl.when(has_next)(z_w.wait_recv)
    for i in range(MASSIVE):
        right[last, i, own] = source_ref[last, i] + w_got[i]
    halo_start(right_copies[last])
    halo_start(rest_copies)
    for n in range(last - 1, -1, -1):
        halo_start(inv_copies[n])
    halo_start(inv_copies[coarse])

    def sweep(src, dst, rhs, factor, edge, shift):
        def body(p, carry):
            x = [src[i, p] for i in range(FIELDS)]
            for i in range(FIELDS):
                vertical = src[i, p - 1] + src[i, p + 1]
                sides = (
                    jnp.where(row > 0, pltpu.roll(x[i], 1, 0), 0.0)
                    + jnp.where(row < 7, pltpu.roll(x[i], 7, 0), 0.0)
                    + jnp.where(col > 0, pltpu.roll(x[i], 1, 1), 0.0)
                    + jnp.where(col < 127, pltpu.roll(x[i], 127, 1), 0.0)
                )
                total = rhs[i, p] + (operator_scale * fibre_weight * diffusion[i]) * vertical
                total = total + (operator_scale * diffusion[i]) * sides
                for j in range(FIELDS):
                    if j != i:
                        total = total + (operator_scale * reaction[j][i]) * x[j]
                dst[i, p - shift] = total * factor[i, p]
            return carry

        lax.fori_loop(edge, wide - edge, body, 0, unroll=True)

    def solve(rhs, factor, result):
        def begin(p, carry):
            for i in range(FIELDS):
                xa[i, p] = rhs[i, p] * factor[i, p]
            return carry

        lax.fori_loop(0, wide, begin, 0, unroll=True)
        sweep(xa, xb, rhs, factor, 1, 0)
        sweep(xb, xa, rhs, factor, 2, 0)
        sweep(xa, xb, rhs, factor, 3, 0)
        sweep(xb, result, rhs, factor, 4, SWEEPS)

    for n in range(last, -1, -1):
        halo_wait(inv_copies[n])
        halo_wait(right_copies[n])
        if n == last - 1:
            halo_wait(rest_copies)
        solve(right.at[n], inv.at[n], adj.at[n])
        if n == last:
            pl.when(has_next)(z_g.wait_recv)
        if n > 0:
            for i in range(MASSIVE):
                before = g_got[i] if n == last else adj[n + 1, i]
                right[n - 1, i, own] = source_ref[n - 1, i] + (4.0 * adj[n, i] - before)
            halo_start(right_copies[n - 1])
        if n == 1:
            halo_wait(inv_copies[coarse])

            @pl.when(t == tms - 1)
            def _():
                solve(rel_right, inv.at[coarse], zero_q)

        if n == 0:
            for i in range(MASSIVE):
                rel_src[i] = adj[0, i] - 0.25 * adj[1, i]

            @pl.when(has_prev)
            def _():
                z_rel.start()
                z_rel_p0.start()

        for i in range(FIELDS):
            term = adj[n, i] * states_ref[n, i].astype(jnp.float32)
            spot = pl.ds(i * thick, thick)
            part[spot] = term if n == last else part[spot] + term

    def send_corrected():
        for i in range(MASSIVE):
            cor_src[i] = cor[0, i] - 0.25 * cor[1, i]

        @pl.when(has_prev)
        def _():
            z_cor.start()
            z_cor_p0.start()

    @pl.when(t == tms - 1)
    def _():
        for i in range(FIELDS):
            zero_p1 = 0.5 * (zero_q[i] + 0.0)
            cor[0, i] = zero_q[i] + (adj[0, i] - zero_q[i])
            cor[1, i] = zero_p1 + (adj[1, i] - zero_p1)
        send_corrected()

    chunk = FIELDS * thick // tms
    grad_one, grad_two, grad_in = [], [], []
    for hop in range(1, tms):
        target = lax.rem(t + hop, tms)
        origin = lax.rem(t + tms - hop, tms)
        grad_one.append(
            pltpu.make_async_remote_copy(
                part.at[pl.ds(target * chunk, chunk)], part_got.at[hop - 1],
                grad_send.at[0, hop - 1], grad_recv.at[0, hop - 1],
                device_id={"tm": target}, device_id_type=MESH,
            )
        )
        mine = whole.at[pl.ds(t * chunk, chunk)]
        grad_two.append(
            pltpu.make_async_remote_copy(
                mine, mine, grad_send.at[1, hop - 1], grad_recv.at[1, hop - 1],
                device_id={"tm": target}, device_id_type=MESH,
            )
        )
        theirs = whole.at[pl.ds(origin * chunk, chunk)]
        grad_in.append(
            pltpu.make_async_remote_copy(
                theirs, theirs, grad_send.at[1, hop - 1], grad_recv.at[1, hop - 1],
                device_id={"tm": target}, device_id_type=MESH,
            )
        )
    for copy in grad_one:
        copy.start()

    def take_corrected():
        z_cor.wait_recv()
        halo_start(cor_copies)

    @pl.when(has_next)
    def _():
        z_rel.wait_recv()
        halo_start(rel_copies)

        @pl.when(t == tms - 2)
        def _():
            take_corrected()

        halo_wait(rel_copies)
        solve(rel_right, inv.at[coarse], rel_q)
        z_rel_p0.wait_recv()
        for i in range(FIELDS):
            offs[0, i] = adj[0, i] - rel_q[i]
            offs[1, i] = adj[1, i] - 0.5 * (rel_q[i] + rel_p0[i])

    for copy in grad_one:
        copy.wait_recv()
    total = part[pl.ds(t * chunk, chunk)]
    for hop in range(1, tms):
        total = total + part_got[hop - 1]
    whole[pl.ds(t * chunk, chunk)] = time_step * total
    for copy in grad_two:
        copy.start()

    @pl.when(has_next)
    def _():
        @pl.when(t < tms - 2)
        def _():
            take_corrected()

        halo_wait(cor_copies)
        solve(cor_right, inv.at[coarse], cor_q)
        z_cor_p0.wait_recv()
        for i in range(FIELDS):
            cor[0, i] = cor_q[i] + offs[0, i]
            cor[1, i] = 0.5 * (cor_q[i] + cor_p0[i]) + offs[1, i]
        send_corrected()

    for pair in range(2):
        corrected_ref[0, pair] = cor[pair]
    for copy in grad_in:
        copy.wait_recv()
    for i in range(FIELDS):
        gradient_ref[i] = whole[pl.ds(i * thick, thick)]

    for copies in inv_copies + right_copies + [rest_copies]:
        halo_sent(copies)

    @pl.when(has_next)
    def _():
        halo_sent(rel_copies)
        halo_sent(cor_copies)

    @pl.when(has_prev)
    def _():
        for copy in (z_w, z_g, z_rel, z_rel_p0, z_cor, z_cor_p0):
            copy.wait_send()

    for copy in grad_one + grad_two:
        copy.wait_send()


def on_device(tms, spaces, forward_states, adjoint_source, source_gain, guess_pairs):
    steps, _, thick = forward_states.shape[:3]
    wide = thick + 2 * SWEEPS
    vmem = lambda *shape: pltpu.VMEM(shape + (8, 128), jnp.float32)
    chunk = FIELDS * thick // tms
    in_vmem = pl.BlockSpec(memory_space=pltpu.VMEM)
    return pl.pallas_call(
        functools.partial(kernel, steps, thick, tms, spaces),
        out_shape=(
            jax.ShapeDtypeStruct(guess_pairs.shape, jnp.float32),
            jax.ShapeDtypeStruct(source_gain.shape, jnp.float32),
        ),
        in_specs=[in_vmem] * 4,
        out_specs=(in_vmem, in_vmem),
        scratch_shapes=[
            vmem(steps + 1, FIELDS, wide),
            vmem(steps, FIELDS, wide),
            vmem(FIELDS, wide),
            vmem(FIELDS, wide),
            vmem(FIELDS, wide),
            vmem(FIELDS, wide),
            vmem(steps, FIELDS, thick),
            vmem(FIELDS, thick),
            vmem(FIELDS, thick),
            vmem(FIELDS, thick),
            vmem(2, FIELDS, thick),
            vmem(2, FIELDS, thick),
            vmem(MASSIVE, thick),
            vmem(MASSIVE, thick),
            vmem(MASSIVE, thick),
            vmem(MASSIVE, thick),
            vmem(MASSIVE, thick),
            vmem(FIELDS, thick),
            vmem(MASSIVE, thick),
            vmem(FIELDS, thick),
            vmem(FIELDS * thick),
            vmem(tms - 1, chunk),
            vmem(FIELDS * thick),
            pltpu.SemaphoreType.DMA((2 * steps + 4, 2)),
            pltpu.SemaphoreType.DMA((2 * steps + 4, 2)),
            pltpu.SemaphoreType.DMA((6,)),
            pltpu.SemaphoreType.DMA((6,)),
            pltpu.SemaphoreType.DMA((2, tms - 1)),
            pltpu.SemaphoreType.DMA((2, tms - 1)),
        ],
        compiler_params=pltpu.CompilerParams(
            collective_id=0, has_side_effects=True, vmem_limit_bytes=32 * 1024 * 1024
        ),
        name="adjoint_cycle",
    )(forward_states, adjoint_source, source_gain, guess_pairs)


def solution(mesh):
    placed = (
        P("tm", None, "space", None, None),
        P("tm", None, "space", None, None),
        P(None, "space", None, None),
        P("tm", None, None, "space", None, None),
    )
    return jax.shard_map(
        functools.partial(on_device, mesh.shape["tm"], mesh.shape["space"]),
        mesh=mesh,
        in_specs=placed,
        out_specs=(P("tm", None, None, "space", None, None), P(None, "space", None, None)),
        check_vma=False,
    )
```

time: 187 us -> 51.3 us (0.27); the launches traced: 185 us -> 51.1 us
  waiting for transfers between devices: 85.4 us -> 0 us
  starting transfers between devices: 64 us -> 0 us
  Pallas kernels: 0 us -> 45.6 us
  between operations: 15.2 us -> 0.65 us
  other arithmetic: 11.6 us -> 0 us
  local copies, waits for them, and re-layouts: 7.76 us -> 4.88 us
    ppermute x24 -> x0, starting transfers between devices: 64 us -> none  [the longest x9 28.8 us: with_halo(): lax.ppermute(tail, axis, [(i, (i + 1) % count) for i in range(ends)])]
    ppermute x24 -> x0, waiting for transfers between devices: 60.2 us -> none  [the longest x6 28.2 us: passed_along(): lax.ppermute(value, axis, [(source, source + steps) for source in range(i...]
    pallas_call x0 -> x1, Pallas kernels: none -> 45.6 us  [on_device(): pl.pallas_call(functools.partial(kernel, steps, thick, tms, spaces), out_...]
    psum x1 -> x0, waiting for transfers between devices: 25.2 us -> none  [on_device(): gradient = lax.psum(time_step * running, 'tm')]
    slice x113 -> x0, local copies, waits for them, and re-layouts: 6.28 us -> none  [the longest x108 5.91 us: from_below(): retained = lax.slice_in_dim(field, 0, extent - 1, axis=axis)]
    select_n x36 -> x0, other arithmetic: 5.44 us -> none  [the longest x27 4.53 us: relax(): jnp.where(inside, jacobi_sweep(iterate, wide_right, safe_diagonal), 0.0)]
    unnamed x17 -> x10, local copies, waits for them, and re-layouts: 1.35 us -> 4.88 us
    add x45 -> x0, other arithmetic: 2.13 us -> none  [the longest x36 1.44 us: coupling(): running = running + reaction[source][target] * field[source]]
  transfers between devices with their start and end apart: 25 -> 0, of which waited for: 20 -> 0; matrix products, arithmetic and copies ran while one was open for 2% -> 0% of each run, Pallas kernels for 0% -> 0%
where the time goes in v1:
time: 51.3 us; the launch traced here: 51.1 us
  Pallas kernels  45.6 us (89%)
  local copies, waits for them, and re-layouts  4.88 us (10%)
  between operations  0.65 us (1%)
    pallas_call x1, Pallas kernels, on_device(): pl.pallas_call(functools.partial(kernel, steps, thick, tms, spaces), out_...  45.6 us
    unnamed x10, local copies, waits for them, and re-layouts  4.88 us

profile of v1, /device:TPU:3, one launch (start us, length us, event | category | flops | bytes accessed | tf_op | source)
XLA Modules:
  0.0 51.1 jit_solution(6390525594270219155)
XLA Ops:
  0.6 0.0 copy-start
  0.6 0.9 %copy-done = f32[4,4,4,8,128]{4,3,2,1,0:T(8,128)S(1)} copy-done((f32[4,4,4,8,128]{4,3,2,1,0:T(8,128)S(1)}, f32[4,4,4,8,128]{4,3,2,1,0:T(8,128)}, u32[]{:S(2)}) %copy-start) | copy-done | bytes 262168
  1.6 0.0 copy-start.1
  1.6 0.9 %copy-done.1 = bf16[4,4,4,8,128]{4,3,2,1,0:T(8,128)(2,1)S(1)} copy-done((bf16[4,4,4,8,128]{4,3,2,1,0:T(8,128)(2,1)S(1)}, bf16[4,4,4,8,128]{4,3,2,1,0:T(8,128)(2,1)}, u32[]{:S(2)}) %copy-start.1) | copy-done | bytes 131096
  2.5 0.0 copy-start.2
  2.5 0.9 %copy-done.2 = f32[1,2,4,4,8,128]{5,4,3,2,1,0:T(8,128)S(1)} copy-done((f32[1,2,4,4,8,128]{5,4,3,2,1,0:T(8,128)S(1)}, f32[1,2,4,4,8,128]{5,4,3,2,1,0:T(8,128)}, u32[]{:S(2)}) %copy-start.2) | copy-done | bytes 131096
  3.4 0.0 copy-start.3
  3.4 0.8 %copy-done.3 = f32[4,4,8,128]{3,2,1,0:T(8,128)S(1)} copy-done((f32[4,4,8,128]{3,2,1,0:T(8,128)S(1)}, f32[4,4,8,128]{3,2,1,0:T(8,128)}, u32[]{:S(2)}) %copy-start.3) | copy-done | bytes 65560
  4.2 45.6 %adjoint_cycle.1 = (f32[1,2,4,4,8,128]{5,4,3,2,1,0:T(8,128)S(1)}, f32[4,4,8,128]{3,2,1,0:T(8,128)S(1)}) custom-call(bf16[4,4,4,8,128]{4,3,2,1,0:T(8,128)(2,1)S(1)} %copy-done.1, f32[4,4,4,8,128]{4,3,2,1,0:T(8,128)S(1)} %copy-done, f32[4,4,8,128]{3,2,1,0:T(8,128)S(1)} %copy-done.3, f32[1,2,4,4,8,128]{5,4,3,2,1,0:T(8,128)S(1)} %copy-done.2), custom_call_target="tpu_custom_call" | custom-call | tf_op jit(solution)/shard_map/adjoint_cycle/pallas_call | solution.py:371
  49.8 0.7 %copy.8 = f32[1,2,4,4,8,128]{5,4,3,2,1,0:T(8,128)} copy(f32[1,2,4,4,8,128]{5,4,3,2,1,0:T(8,128)S(1)} %get-tuple-element.4) | data formatting | bytes 262144
  50.5 0.6 %copy.9 = f32[4,4,8,128]{3,2,1,0:T(8,128)} copy(f32[4,4,8,128]{3,2,1,0:T(8,128)S(1)} %get-tuple-element.5) | data formatting | bytes 131072
Async XLA Ops:
  0.6 1.0 %copy-start = (f32[4,4,4,8,128]{4,3,2,1,0:T(8,128)S(1)}, f32[4,4,4,8,128]{4,3,2,1,0:T(8,128)}, u32[]{:S(2)}) copy-start(f32[4,4,4,8,128]{4,3,2,1,0:T(8,128)} %source_ref.1) | copy-start | bytes 786436
  1.6 0.9 %copy-start.1 = (bf16[4,4,4,8,128]{4,3,2,1,0:T(8,128)(2,1)S(1)}, bf16[4,4,4,8,128]{4,3,2,1,0:T(8,128)(2,1)}, u32[]{:S(2)}) copy-start(bf16[4,4,4,8,128]{4,3,2,1,0:T(8,128)(2,1)} %states_ref.1) | copy-start | bytes 393220
  2.5 0.9 %copy-start.2 = (f32[1,2,4,4,8,128]{5,4,3,2,1,0:T(8,128)S(1)}, f32[1,2,4,4,8,128]{5,4,3,2,1,0:T(8,128)}, u32[]{:S(2)}) copy-start(f32[1,2,4,4,8,128]{5,4,3,2,1,0:T(8,128)} %guess_ref.1) | copy-start | bytes 393220
  3.4 0.8 %copy-start.3 = (f32[4,4,8,128]{3,2,1,0:T(8,128)S(1)}, f32[4,4,8,128]{3,2,1,0:T(8,128)}, u32[]{:S(2)}) copy-start(f32[4,4,8,128]{3,2,1,0:T(8,128)} %gain_ref.1) | copy-start | bytes 196612

commit v2 on v1

v2 whole, which is shorter than its diff:
```python
import functools

import jax
import jax.numpy as jnp
from jax import lax
from jax.experimental import pallas as pl
from jax.experimental.pallas import tpu as pltpu
from jax.sharding import PartitionSpec as P

SWEEPS = 4
FIELDS = 4
MASSIVE = 3

diffusion = (2.4, 1.2, 0.6, 4.0)
fibre_weight = 128.0
reaction = (
    (-14.4, 7.2, -4.8, 2.4),
    (4.8, -19.2, 7.2, -4.8),
    (-7.2, 2.4, -12.0, 7.2),
    (4.8, -7.2, 2.4, -38.4),
)
self_rates = (-14.4, -19.2, -12.0, -38.4)
masses = (1.0, 1.0, 1.0, 0.0)
fine_rate = 3.0
coarse_rate = 0.75
time_step = 0.5
operator_scale = 0.0078125
state_weight = 0.1
gain_weight = 0.25

MESH = pl.DeviceIdType.MESH


def kernel(
    steps, thick, tms, spaces,
    states_hbm, source_hbm, gain_hbm, guess_hbm,
    corrected_ref, gradient_ref,
    states_ref, source_ref, gain_ref, guess_ref,
    inv, inv_turned, right, right_turned, w_right, rel_right, cor_right, xs,
    adj, zero_q, rel_q, cor_q, offs, cor,
    w_src, w_turned, g_src, g_got, rel_src, rel_turned, rel_p0, cor_src, cor_turned, cor_p0,
    passed_on, part, part_got, whole,
    load_sem, halo_send, halo_recv, z_send, z_recv, grad_send, grad_recv,
):
    t = lax.axis_index("tm")
    s = lax.axis_index("space")
    odd = lax.rem(s, 2)
    sibling = s + 1 - 2 * odd
    other = s - 1 + 2 * odd
    has_other = jnp.logical_and(other >= 0, other < spaces)
    has_next, has_prev = t < tms - 1, t > 0
    wide = thick + 2 * SWEEPS
    first, end = SWEEPS, SWEEPS + thick
    own = pl.ds(SWEEPS, thick)
    low = pl.ds(0, SWEEPS)
    high = pl.ds(SWEEPS + thick, SWEEPS)
    heavy = pl.ds(0, MASSIVE)
    coarse = steps
    last = steps - 1
    row = lax.broadcasted_iota(jnp.int32, (8, 128), 0)
    col = lax.broadcasted_iota(jnp.int32, (8, 128), 1)
    place = [p + odd * (thick - 1 - 2 * p) for p in range(thick)]

    loads = [
        pltpu.make_async_copy(hbm, ref, load_sem.at[k])
        for k, (hbm, ref) in enumerate(
            (
                (guess_hbm, guess_ref),
                (states_hbm, states_ref),
                (gain_hbm, gain_ref),
                (source_hbm, source_ref),
            )
        )
    ]
    for load in loads:
        load.start()

    def to_sibling(index, src, dst):
        return pltpu.make_async_remote_copy(
            src, dst, halo_send.at[index, 0], halo_recv.at[index, 0],
            device_id={"space": sibling}, device_id_type=MESH,
        )

    def halo_copies(index, src, view):
        off = pltpu.make_async_remote_copy(
            src, view(low), halo_send.at[index, 1], halo_recv.at[index, 1],
            device_id={"space": other}, device_id_type=MESH,
        )
        return to_sibling(index, src, view(high)), off

    def halo_start(copies):
        pl.when(has_other)(copies[1].start)
        copies[0].start()

    def to_previous(index, src, dst):
        return pltpu.make_async_remote_copy(
            src, dst, z_send.at[index], z_recv.at[index],
            device_id={"tm": t - 1}, device_id_type=MESH,
        )

    def spread_copies(index, halo_index, src, turned, wide_ref):
        straight = to_previous(index, src, wide_ref.at[heavy, own])
        across = pltpu.make_async_remote_copy(
            turned, wide_ref.at[heavy, low], z_send.at[index + 1], z_recv.at[index + 1],
            device_id={"tm": t - 1, "space": other}, device_id_type=MESH,
        )
        onward = to_sibling(halo_index, passed_on.at[index // 2], wide_ref.at[heavy, high])
        return straight, across, onward

    inv_copies = [
        halo_copies(n, inv_turned.at[n], lambda p, n=n: inv.at[n, :, p])
        for n in range(steps + 1)
    ]
    right_copies = [
        halo_copies(steps + 1 + n, right_turned.at[n], lambda p, n=n: right.at[n, :, p])
        if n == last
        else halo_copies(
            steps + 1 + n, right_turned.at[n, heavy], lambda p, n=n: right.at[n, heavy, p]
        )
        for n in range(steps)
    ]
    rest_copies = halo_copies(
        2 * steps + 1,
        right_turned.at[pl.ds(0, last), MASSIVE],
        lambda p: right.at[pl.ds(0, last), MASSIVE, p],
    )
    w_copies = spread_copies(0, 2 * steps + 2, w_src, w_turned, w_right)
    rel_copies = spread_copies(2, 2 * steps + 3, rel_src, rel_turned, rel_right)
    cor_copies = spread_copies(4, 2 * steps + 4, cor_src, cor_turned, cor_right)
    z_g = to_previous(6, g_src, g_got)
    z_rel_p0 = to_previous(7, adj.at[0], rel_p0)
    z_cor_p0 = to_previous(8, cor.at[0], cor_p0)

    rel_right[...] = jnp.zeros_like(rel_right)
    cor_right[...] = jnp.zeros_like(cor_right)

    @pl.when(jnp.logical_not(has_other))
    def _():
        inv[:, :, low] = jnp.zeros((steps + 1, FIELDS, SWEEPS, 8, 128), jnp.float32)
        right[:, :, low] = jnp.zeros((steps, FIELDS, SWEEPS, 8, 128), jnp.float32)
        w_right[:, low] = jnp.zeros((MASSIVE, SWEEPS, 8, 128), jnp.float32)

    @pl.when(t == tms - 1)
    def _():
        w_right[...] = jnp.zeros_like(w_right)
        g_got[...] = jnp.zeros_like(g_got)

    barrier = pltpu.get_barrier_semaphore()

    def greet(**device):
        pl.semaphore_signal(barrier, inc=1, device_id=device, device_id_type=MESH)

    for hop in range(1, tms):
        greet(tm=lax.rem(t + hop, tms))
    greet(space=sibling)

    @pl.when(has_other)
    def _():
        greet(space=other)
        pl.when(has_next)(lambda: greet(tm=t + 1, space=other))
        pl.when(has_prev)(lambda: greet(tm=t - 1, space=other))

    def fill_inverse(slot, n, rate):
        for i in range(FIELDS):
            base = rate * masses[i] + operator_scale * (
                (2.0 * fibre_weight + 4.0) * diffusion[i] - self_rates[i]
            )
            for p in range(thick):
                u = states_ref[n, i, place[p]].astype(jnp.float32)
                diagonal = base + state_weight * u * u - gain_weight * gain_ref[i, place[p]]
                value = 1.0 / diagonal
                inv[slot, i, first + p] = value
                inv_turned[slot, i, thick - 1 - p] = value

    loads[0].wait()
    for i in range(MASSIVE):
        for p in range(thick):
            one = guess_ref[0, 0, i, place[p]]
            value = 4.0 * one - guess_ref[0, 1, i, place[p]]
            w_src[i, p] = value
            w_turned[i, thick - 1 - p] = value
            g_src[i, p] = one
    loads[1].wait()
    loads[2].wait()
    fill_inverse(last, last, fine_rate)
    loads[3].wait()
    for i in range(FIELDS):
        for p in range(thick):
            for n in [last] if i < MASSIVE else range(steps):
                value = source_ref[n, i, place[p]]
                right[n, i, first + p] = value
                right_turned[n, i, thick - 1 - p] = value

    both = has_next.astype(jnp.int32) + has_prev.astype(jnp.int32)
    pl.semaphore_wait(barrier, tms + has_other.astype(jnp.int32) * (1 + both))

    def spread_start(copies):
        @pl.when(has_prev)
        def _():
            copies[0].start()
            pl.when(has_other)(copies[1].start)

    spread_start(w_copies)
    halo_start(inv_copies[last])
    halo_start(right_copies[last])
    pl.when(has_prev)(z_g.start)
    for n in range(last):
        fill_inverse(n, n, fine_rate)
    fill_inverse(coarse, 0, coarse_rate)

    def hand_on(copies, wide_ref, slot):
        copies[0].wait_recv()
        for i in range(MASSIVE):
            for p in range(thick):
                passed_on[slot, i, thick - 1 - p] = wide_ref[i, first + p]
        copies[2].start()

    def add_w(start):
        for i in range(MASSIVE):
            span = pl.ds(start, SWEEPS)
            right[last, i, span] = right[last, i, span] + w_right[i, span]

    def begin(rhs, factor, start, stop):
        def body(p, carry):
            for i in range(FIELDS):
                xs[0, i, p] = rhs[i, p] * factor[i, p]
            return carry

        lax.fori_loop(start, stop, body, 0, unroll=True)

    def sweep(number, rhs, factor, start, stop, result=None):
        src = xs.at[number - 1]

        def body(p, carry):
            x = [src[i, p] for i in range(FIELDS)]
            for i in range(FIELDS):
                vertical = src[i, p - 1] + src[i, p + 1]
                sides = (
                    jnp.where(row > 0, pltpu.roll(x[i], 1, 0), 0.0)
                    + jnp.where(row < 7, pltpu.roll(x[i], 7, 0), 0.0)
                    + jnp.where(col > 0, pltpu.roll(x[i], 1, 1), 0.0)
                    + jnp.where(col < 127, pltpu.roll(x[i], 127, 1), 0.0)
                )
                total = rhs[i, p] + (operator_scale * fibre_weight * diffusion[i]) * vertical
                total = total + (operator_scale * diffusion[i]) * sides
                for j in range(FIELDS):
                    if j != i:
                        total = total + (operator_scale * reaction[j][i]) * x[j]
                if result is None:
                    xs[number, i, p] = total * factor[i, p]
                else:
                    result[i, p - first] = total * factor[i, p]
            return carry

        lax.fori_loop(start, stop, body, 0, unroll=True)

    def solve(rhs, factor, result, near, far):
        begin(rhs, factor, first, end)
        sweep(1, rhs, factor, first + 1, end - 1)
        near()
        begin(rhs, factor, end, wide)
        for number in range(1, SWEEPS):
            start = end - 1 if number == 1 else first + number
            sweep(number, rhs, factor, start, wide - number)
        far()
        begin(rhs, factor, 0, first)
        for number in range(1, SWEEPS):
            sweep(number, rhs, factor, number, first + number)
        sweep(SWEEPS, rhs, factor, first, end, result)

    def wait_other(copies):
        pl.when(has_other)(copies[1].wait_recv)

    for n in range(last, -1, -1):
        if n == last:
            halo_start(inv_copies[n - 1])
            halo_start(rest_copies)

            @pl.when(has_next)
            def _():
                hand_on(w_copies, w_right, 0)

            add_w(first)
        elif n == last - 1:
            for m in range(n):
                halo_start(inv_copies[n - 1 - m])
        elif n == last - 2:
            halo_start(inv_copies[coarse])
        if n == 0:
            inv_copies[coarse][0].wait_recv()
            wait_other(inv_copies[coarse])

            @pl.when(t == tms - 1)
            def _():
                solve(rel_right, inv.at[coarse], zero_q, lambda: None, lambda: None)

        def near(n=n):
            inv_copies[n][0].wait_recv()
            if n == last - 1:
                rest_copies[0].wait_recv()
            right_copies[n][0].wait_recv()
            if n == last:
                pl.when(has_next)(w_copies[2].wait_recv)
                add_w(end)

        def far(n=n):
            wait_other(inv_copies[n])
            if n == last - 1:
                wait_other(rest_copies)
            wait_other(right_copies[n])
            if n == last:
                pl.when(jnp.logical_and(has_next, has_other))(w_copies[1].wait_recv)
                add_w(0)

        solve(right.at[n], inv.at[n], adj.at[n], near, far)
        if n == last:
            pl.when(has_next)(z_g.wait_recv)
        if n > 0:
            for i in range(MASSIVE):
                for p in range(thick):
                    before = g_got[i, p] if n == last else adj[n + 1, i, p]
                    value = source_ref[n - 1, i, place[p]] + (4.0 * adj[n, i, p] - before)
                    right[n - 1, i, first + p] = value
                    right_turned[n - 1, i, thick - 1 - p] = value
            halo_start(right_copies[n - 1])
        else:
            for i in range(MASSIVE):
                for p in range(thick):
                    value = adj[0, i, p] - 0.25 * adj[1, i, p]
                    rel_src[i, p] = value
                    rel_turned[i, thick - 1 - p] = value
            spread_start(rel_copies)

            @pl.when(jnp.logical_and(has_prev, has_next))
            def _():
                z_rel_p0.start()

    def send_corrected():
        for i in range(MASSIVE):
            for p in range(thick):
                value = cor[0, i, p] - 0.25 * cor[1, i, p]
                cor_src[i, p] = value
                cor_turned[i, thick - 1 - p] = value
        spread_start(cor_copies)

    @pl.when(t == tms - 1)
    def _():
        for i in range(FIELDS):
            zero_p1 = 0.5 * (zero_q[i] + 0.0)
            cor[0, i] = zero_q[i] + (adj[0, i] - zero_q[i])
            cor[1, i] = zero_p1 + (adj[1, i] - zero_p1)
        send_corrected()

        @pl.when(has_prev)
        def _():
            z_rel_p0.start()
            z_cor_p0.start()

    for n in range(last, -1, -1):
        for i in range(FIELDS):
            for p in range(thick):
                term = adj[n, i, p] * states_ref[n, i, place[p]].astype(jnp.float32)
                spot = i * thick + p
                part[spot] = term if n == last else part[spot] + term

    chunk = FIELDS * thick // tms
    grad_one, grad_two, grad_in = [], [], []
    for hop in range(1, tms):
        target = lax.rem(t + hop, tms)
        origin = lax.rem(t + tms - hop, tms)
        grad_one.append(
            pltpu.make_async_remote_copy(
                part.at[pl.ds(target * chunk, chunk)], part_got.at[hop - 1],
                grad_send.at[0, hop - 1], grad_recv.at[0, hop - 1],
                device_id={"tm": target}, device_id_type=MESH,
            )
        )
        mine = whole.at[pl.ds(t * chunk, chunk)]
        grad_two.append(
            pltpu.make_async_remote_copy(
                mine, mine, grad_send.at[1, hop - 1], grad_recv.at[1, hop - 1],
                device_id={"tm": target}, device_id_type=MESH,
            )
        )
        theirs = whole.at[pl.ds(origin * chunk, chunk)]
        grad_in.append(
            pltpu.make_async_remote_copy(
                theirs, theirs, grad_send.at[1, hop - 1], grad_recv.at[1, hop - 1],
                device_id={"tm": target}, device_id_type=MESH,
            )
        )
    for copy in grad_one:
        copy.start()

    @pl.when(has_next)
    def _():
        hand_on(rel_copies, rel_right, 1)

        @pl.when(t == tms - 2)
        def _():
            hand_on(cor_copies, cor_right, 2)

        def far():
            pl.when(has_other)(rel_copies[1].wait_recv)

        solve(rel_right, inv.at[coarse], rel_q, rel_copies[2].wait_recv, far)
        z_rel_p0.wait_recv()
        for i in range(FIELDS):
            offs[0, i] = adj[0, i] - rel_q[i]
            offs[1, i] = adj[1, i] - 0.5 * (rel_q[i] + rel_p0[i])

    def share_gradient():
        for copy in grad_one:
            copy.wait_recv()
        total = part[pl.ds(t * chunk, chunk)]
        for hop in range(1, tms):
            total = total + part_got[hop - 1]
        whole[pl.ds(t * chunk, chunk)] = time_step * total
        for copy in grad_two:
            copy.start()

    pl.when(jnp.logical_or(t < tms - 2, t == tms - 1))(share_gradient)

    @pl.when(has_next)
    def _():
        @pl.when(t < tms - 2)
        def _():
            hand_on(cor_copies, cor_right, 2)

        def far():
            pl.when(has_other)(cor_copies[1].wait_recv)

        solve(cor_right, inv.at[coarse], cor_q, cor_copies[2].wait_recv, far)
        z_cor_p0.wait_recv()
        for i in range(FIELDS):
            cor[0, i] = cor_q[i] + offs[0, i]
            cor[1, i] = 0.5 * (cor_q[i] + cor_p0[i]) + offs[1, i]
        send_corrected()
        pl.when(has_prev)(z_cor_p0.start)

    pl.when(t == tms - 2)(share_gradient)

    for pair in range(2):
        for i in range(FIELDS):
            for p in range(thick):
                corrected_ref[0, pair, i, place[p]] = cor[pair, i, p]
    for copy in grad_in:
        copy.wait_recv()
    for i in range(FIELDS):
        for p in range(thick):
            gradient_ref[i, place[p]] = whole[i * thick + p]

    halos = inv_copies + right_copies + [rest_copies]
    for copies in halos:
        copies[0].wait_send()

    @pl.when(has_other)
    def _():
        for copies in halos:
            copies[1].wait_send()

    @pl.when(has_next)
    def _():
        for copies in (w_copies, rel_copies, cor_copies):
            copies[2].wait_send()

    @pl.when(has_prev)
    def _():
        for copies in (w_copies, rel_copies, cor_copies):
            copies[0].wait_send()
            pl.when(has_other)(copies[1].wait_send)
        for copy in (z_g, z_rel_p0, z_cor_p0):
            copy.wait_send()

    for copy in grad_one + grad_two:
        copy.wait_send()


def on_device(tms, spaces, forward_states, adjoint_source, source_gain, guess_pairs):
    steps, _, thick = forward_states.shape[:3]
    wide = thick + 2 * SWEEPS
    vmem = lambda *shape: pltpu.VMEM(shape + (8, 128), jnp.float32)
    chunk = FIELDS * thick // tms
    in_vmem = pl.BlockSpec(memory_space=pltpu.VMEM)
    heavy = vmem(MASSIVE, thick)
    every = vmem(FIELDS, thick)
    return pl.pallas_call(
        functools.partial(kernel, steps, thick, tms, spaces),
        out_shape=(
            jax.ShapeDtypeStruct(guess_pairs.shape, jnp.float32),
            jax.ShapeDtypeStruct(source_gain.shape, jnp.float32),
        ),
        in_specs=[pl.BlockSpec(memory_space=pl.ANY)] * 4,
        out_specs=(in_vmem, in_vmem),
        scratch_shapes=[
            pltpu.VMEM(forward_states.shape, forward_states.dtype),
            pltpu.VMEM(adjoint_source.shape, jnp.float32),
            pltpu.VMEM(source_gain.shape, jnp.float32),
            pltpu.VMEM(guess_pairs.shape, jnp.float32),
            vmem(steps + 1, FIELDS, wide),
            vmem(steps + 1, FIELDS, thick),
            vmem(steps, FIELDS, wide),
            vmem(steps, FIELDS, thick),
            vmem(MASSIVE, wide),
            vmem(FIELDS, wide),
            vmem(FIELDS, wide),
            vmem(SWEEPS, FIELDS, wide),
            vmem(steps, FIELDS, thick),
            every,
            every,
            every,
            vmem(2, FIELDS, thick),
            vmem(2, FIELDS, thick),
            heavy,
            heavy,
            heavy,
            heavy,
            heavy,
            heavy,
            every,
            heavy,
            heavy,
            every,
            vmem(3, MASSIVE, thick),
            vmem(FIELDS * thick),
            vmem(tms - 1, chunk),
            vmem(FIELDS * thick),
            pltpu.SemaphoreType.DMA((4,)),
            pltpu.SemaphoreType.DMA((2 * steps + 5, 2)),
            pltpu.SemaphoreType.DMA((2 * steps + 5, 2)),
            pltpu.SemaphoreType.DMA((9,)),
            pltpu.SemaphoreType.DMA((9,)),
            pltpu.SemaphoreType.DMA((2, tms - 1)),
            pltpu.SemaphoreType.DMA((2, tms - 1)),
        ],
        compiler_params=pltpu.CompilerParams(
            collective_id=0, has_side_effects=True, vmem_limit_bytes=32 * 1024 * 1024
        ),
        name="adjoint_cycle",
    )(forward_states, adjoint_source, source_gain, guess_pairs)


def solution(mesh):
    placed = (
        P("tm", None, "space", None, None),
        P("tm", None, "space", None, None),
        P(None, "space", None, None),
        P("tm", None, None, "space", None, None),
    )
    return jax.shard_map(
        functools.partial(on_device, mesh.shape["tm"], mesh.shape["space"]),
        mesh=mesh,
        in_specs=placed,
        out_specs=(P("tm", None, None, "space", None, None), P(None, "space", None, None)),
        check_vma=False,
    )
```

time: 51.3 us -> 46.4 us (0.904)
  Pallas kernels: 45.6 us -> 40.6 us
    pallas_call x1, Pallas kernels: 45.6 us -> 40.6 us  [on_device(): pl.pallas_call(functools.partial(kernel, steps, thick, tms, spaces), out_...]
where the time goes in v2:
time: 46.4 us; the launch traced here: 46.1 us
  Pallas kernels  40.6 us (88%)
  local copies, waits for them, and re-layouts  4.88 us (11%)
  between operations  0.65 us (1%)
    pallas_call x1, Pallas kernels, on_device(): pl.pallas_call(functools.partial(kernel, steps, thick, tms, spaces), out_...  40.6 us
    unnamed x10, local copies, waits for them, and re-layouts  4.88 us

profile of v2, /device:TPU:3, one launch (start us, length us, event | category | flops | bytes accessed | tf_op | source)
XLA Modules:
  0.0 46.1 jit_solution(229568659974139984)
XLA Ops:
  0.6 0.0 copy-start
  0.6 0.9 %copy-done = f32[4,4,4,8,128]{4,3,2,1,0:T(8,128)S(1)} copy-done((f32[4,4,4,8,128]{4,3,2,1,0:T(8,128)S(1)}, f32[4,4,4,8,128]{4,3,2,1,0:T(8,128)}, u32[]{:S(2)}) %copy-start) | copy-done | bytes 262168
  1.6 0.0 copy-start.1
  1.6 0.9 %copy-done.1 = bf16[4,4,4,8,128]{4,3,2,1,0:T(8,128)(2,1)S(1)} copy-done((bf16[4,4,4,8,128]{4,3,2,1,0:T(8,128)(2,1)S(1)}, bf16[4,4,4,8,128]{4,3,2,1,0:T(8,128)(2,1)}, u32[]{:S(2)}) %copy-start.1) | copy-done | bytes 131096
  2.5 0.0 copy-start.2
  2.5 0.9 %copy-done.2 = f32[1,2,4,4,8,128]{5,4,3,2,1,0:T(8,128)S(1)} copy-done((f32[1,2,4,4,8,128]{5,4,3,2,1,0:T(8,128)S(1)}, f32[1,2,4,4,8,128]{5,4,3,2,1,0:T(8,128)}, u32[]{:S(2)}) %copy-start.2) | copy-done | bytes 131096
  3.4 0.0 copy-start.3
  3.4 0.8 %copy-done.3 = f32[4,4,8,128]{3,2,1,0:T(8,128)S(1)} copy-done((f32[4,4,8,128]{3,2,1,0:T(8,128)S(1)}, f32[4,4,8,128]{3,2,1,0:T(8,128)}, u32[]{:S(2)}) %copy-start.3) | copy-done | bytes 65560
  4.2 40.6 %adjoint_cycle.1 = (f32[1,2,4,4,8,128]{5,4,3,2,1,0:T(8,128)S(1)}, f32[4,4,8,128]{3,2,1,0:T(8,128)S(1)}) custom-call(bf16[4,4,4,8,128]{4,3,2,1,0:T(8,128)(2,1)S(1)} %copy-done.1, f32[4,4,4,8,128]{4,3,2,1,0:T(8,128)S(1)} %copy-done, f32[4,4,8,128]{3,2,1,0:T(8,128)S(1)} %copy-done.3, f32[1,2,4,4,8,128]{5,4,3,2,1,0:T(8,128)S(1)} %copy-done.2), custom_call_target="tpu_custom_call" | custom-call | tf_op jit(solution)/shard_map/adjoint_cycle/pallas_call | solution.py:487
  44.8 0.7 %copy.8 = f32[1,2,4,4,8,128]{5,4,3,2,1,0:T(8,128)} copy(f32[1,2,4,4,8,128]{5,4,3,2,1,0:T(8,128)S(1)} %get-tuple-element.4) | data formatting | bytes 262144
  45.5 0.6 %copy.9 = f32[4,4,8,128]{3,2,1,0:T(8,128)} copy(f32[4,4,8,128]{3,2,1,0:T(8,128)S(1)} %get-tuple-element.5) | data formatting | bytes 131072
Async XLA Ops:
  0.6 1.0 %copy-start = (f32[4,4,4,8,128]{4,3,2,1,0:T(8,128)S(1)}, f32[4,4,4,8,128]{4,3,2,1,0:T(8,128)}, u32[]{:S(2)}) copy-start(f32[4,4,4,8,128]{4,3,2,1,0:T(8,128)} %source_hbm.1) | copy-start | bytes 786436
  1.6 0.9 %copy-start.1 = (bf16[4,4,4,8,128]{4,3,2,1,0:T(8,128)(2,1)S(1)}, bf16[4,4,4,8,128]{4,3,2,1,0:T(8,128)(2,1)}, u32[]{:S(2)}) copy-start(bf16[4,4,4,8,128]{4,3,2,1,0:T(8,128)(2,1)} %states_hbm.1) | copy-start | bytes 393220
  2.5 0.9 %copy-start.2 = (f32[1,2,4,4,8,128]{5,4,3,2,1,0:T(8,128)S(1)}, f32[1,2,4,4,8,128]{5,4,3,2,1,0:T(8,128)}, u32[]{:S(2)}) copy-start(f32[1,2,4,4,8,128]{5,4,3,2,1,0:T(8,128)} %guess_hbm.1) | copy-start | bytes 393220
  3.4 0.8 %copy-start.3 = (f32[4,4,8,128]{3,2,1,0:T(8,128)S(1)}, f32[4,4,8,128]{3,2,1,0:T(8,128)}, u32[]{:S(2)}) copy-start(f32[4,4,8,128]{3,2,1,0:T(8,128)} %gain_hbm.1) | copy-start | bytes 196612

commit v3 on v2

--- a/solution.py
+++ b/solution.py
@@ -109,7 +109,7 @@
 
     inv_copies = [
         halo_copies(n, inv_turned.at[n], lambda p, n=n: inv.at[n, :, p])
-        for n in range(steps + 1)
+        for n in range(steps)
     ]
     right_copies = [
         halo_copies(steps + 1 + n, right_turned.at[n], lambda p, n=n: right.at[n, :, p])
@@ -170,7 +170,8 @@
                 diagonal = base + state_weight * u * u - gain_weight * gain_ref[i, place[p]]
                 value = 1.0 / diagonal
                 inv[slot, i, first + p] = value
-                inv_turned[slot, i, thick - 1 - p] = value
+                if slot < steps:
+                    inv_turned[slot, i, thick - 1 - p] = diagonal if slot == 0 else value
 
     loads[0].wait()
     for i in range(MASSIVE):
@@ -208,6 +209,13 @@
         fill_inverse(n, n, fine_rate)
     fill_inverse(coarse, 0, coarse_rate)
 
+    def invert_first(start):
+        for i in range(FIELDS):
+            for p in range(start, start + SWEEPS):
+                diagonal = inv[0, i, p]
+                inv[coarse, i, p] = 1.0 / (diagonal - (fine_rate - coarse_rate) * masses[i])
+                inv[0, i, p] = 1.0 / diagonal
+
     def hand_on(copies, wide_ref, slot):
         copies[0].wait_recv()
         for i in range(MASSIVE):
@@ -235,17 +243,20 @@
             x = [src[i, p] for i in range(FIELDS)]
             for i in range(FIELDS):
                 vertical = src[i, p - 1] + src[i, p + 1]
-                sides = (
-                    jnp.where(row > 0, pltpu.roll(x[i], 1, 0), 0.0)
-                    + jnp.where(row < 7, pltpu.roll(x[i], 7, 0), 0.0)
-                    + jnp.where(col > 0, pltpu.roll(x[i], 1, 1), 0.0)
-                    + jnp.where(col < 127, pltpu.roll(x[i], 127, 1), 0.0)
-                )
                 total = rhs[i, p] + (operator_scale * fibre_weight * diffusion[i]) * vertical
-                total = total + (operator_scale * diffusion[i]) * sides
+                mixed = None
                 for j in range(FIELDS):
                     if j != i:
-                        total = total + (operator_scale * reaction[j][i]) * x[j]
+                        term = (operator_scale * reaction[j][i]) * x[j]
+                        mixed = term if mixed is None else mixed + term
+                total = total + mixed
+                along = jnp.where(row > 0, pltpu.roll(x[i], 1, 0), 0.0) + jnp.where(
+                    row < 7, pltpu.roll(x[i], 7, 0), 0.0
+                )
+                across = jnp.where(col > 0, pltpu.roll(x[i], 1, 1), 0.0) + jnp.where(
+                    col < 127, pltpu.roll(x[i], 127, 1), 0.0
+                )
+                total = total + (operator_scale * diffusion[i]) * (along + across)
                 if result is None:
                     xs[number, i, p] = total * factor[i, p]
                 else:
@@ -284,18 +295,22 @@
         elif n == last - 1:
             for m in range(n):
                 halo_start(inv_copies[n - 1 - m])
-        elif n == last - 2:
-            halo_start(inv_copies[coarse])
         if n == 0:
-            inv_copies[coarse][0].wait_recv()
-            wait_other(inv_copies[coarse])
+            inv_copies[0][0].wait_recv()
+            invert_first(end)
+
+            @pl.when(has_other)
+            def _():
+                inv_copies[0][1].wait_recv()
+                invert_first(0)
 
             @pl.when(t == tms - 1)
             def _():
                 solve(rel_right, inv.at[coarse], zero_q, lambda: None, lambda: None)
 
         def near(n=n):
-            inv_copies[n][0].wait_recv()
+            if n > 0:
+                inv_copies[n][0].wait_recv()
             if n == last - 1:
                 rest_copies[0].wait_recv()
             right_copies[n][0].wait_recv()
@@ -304,7 +319,8 @@
                 add_w(end)
 
         def far(n=n):
-            wait_other(inv_copies[n])
+            if n > 0:
+                wait_other(inv_copies[n])
             if n == last - 1:
                 wait_other(rest_copies)
             wait_other(right_copies[n])
@@ -490,7 +506,7 @@
             jax.ShapeDtypeStruct(guess_pairs.shape, jnp.float32),
             jax.ShapeDtypeStruct(source_gain.shape, jnp.float32),
         ),
-        in_specs=[pl.BlockSpec(memory_space=pl.ANY)] * 4,
+        in_specs=[pl.BlockSpec(memory_space=pltpu.HBM)] * 4,
         out_specs=(in_vmem, in_vmem),
         scratch_shapes=[
             pltpu.VMEM(forward_states.shape, forward_states.dtype),
@@ -498,7 +514,7 @@
             pltpu.VMEM(source_gain.shape, jnp.float32),
             pltpu.VMEM(guess_pairs.shape, jnp.float32),
             vmem(steps + 1, FIELDS, wide),
-            vmem(steps + 1, FIELDS, thick),
+            vmem(steps, FIELDS, thick),
             vmem(steps, FIELDS, wide),
             vmem(steps, FIELDS, thick),
             vmem(MASSIVE, wide),
@@ -534,7 +550,7 @@
             pltpu.SemaphoreType.DMA((2, tms - 1)),
         ],
         compiler_params=pltpu.CompilerParams(
-            collective_id=0, has_side_effects=True, vmem_limit_bytes=32 * 1024 * 1024
+            collective_id=0, has_side_effects=True, vmem_limit_bytes=64 * 1024 * 1024
         ),
         name="adjoint_cycle",
     )(forward_states, adjoint_source, source_gain, guess_pairs)

time: 46.4 us -> 43.8 us (0.944)
  local copies, waits for them, and re-layouts: 4.88 us -> 2.23 us
    unnamed x10 -> x4, local copies, waits for them, and re-layouts: 4.88 us -> 2.23 us
where the time goes in v3:
time: 43.8 us; the launch traced here: 43.6 us
  Pallas kernels  40.8 us (93%)
  local copies, waits for them, and re-layouts  2.23 us (5%)
  between operations  0.65 us (1%)
    pallas_call x1, Pallas kernels, on_device(): pl.pallas_call(functools.partial(kernel, steps, thick, tms, spaces), out_...  40.8 us
    unnamed x4, local copies, waits for them, and re-layouts  2.23 us

profile of v3, /device:TPU:3, one launch (start us, length us, event | category | flops | bytes accessed | tf_op | source)
XLA Modules:
  0.0 43.6 jit_solution(15639993992086353448)
XLA Ops:
  0.6 40.8 %adjoint_cycle.1 = (f32[1,2,4,4,8,128]{5,4,3,2,1,0:T(8,128)}, f32[4,4,8,128]{3,2,1,0:T(8,128)}) custom-call(bf16[4,4,4,8,128]{4,3,2,1,0:T(8,128)(2,1)} %states_hbm.1, f32[4,4,4,8,128]{4,3,2,1,0:T(8,128)} %source_hbm.1, f32[4,4,8,128]{3,2,1,0:T(8,128)} %gain_hbm.1, f32[1,2,4,4,8,128]{5,4,3,2,1,0:T(8,128)} %guess_hbm.1), custom_call_target="tpu_custom_call" | custom-call | tf_op jit(solution)/shard_map/adjoint_cycle/pallas_call | solution.py:503
  41.4 0.0 copy-start
  41.4 1.6 %copy.8 = f32[1,2,4,4,8,128]{5,4,3,2,1,0:T(8,128)} copy(f32[1,2,4,4,8,128]{5,4,3,2,1,0:T(8,128)} %get-tuple-element.4) | data formatting | bytes 262144
  43.0 0.0 copy-done
  43.0 0.6 %copy.9 = f32[4,4,8,128]{3,2,1,0:T(8,128)} copy(f32[4,4,8,128]{3,2,1,0:T(8,128)S(1)} %copy-done) | data formatting | bytes 131072
Async XLA Ops:
  41.4 1.6 %copy-start = (f32[4,4,8,128]{3,2,1,0:T(8,128)S(1)}, f32[4,4,8,128]{3,2,1,0:T(8,128)}, u32[]{:S(2)}) copy-start(f32[4,4,8,128]{3,2,1,0:T(8,128)} %get-tuple-element.5) | copy-start | bytes 196612

commit v4 on v3

--- a/solution.py
+++ b/solution.py
@@ -38,7 +38,7 @@
     states_ref, source_ref, gain_ref, guess_ref,
     inv, inv_turned, right, right_turned, w_right, rel_right, cor_right, xs,
     adj, zero_q, rel_q, cor_q, offs, cor,
-    w_src, w_turned, g_src, g_got, rel_src, rel_turned, rel_p0, cor_src, cor_turned, cor_p0,
+    w_src, w_turned, g_src, g_got, rel_src, rel_turned, cor_src, cor_turned, change, change_got,
     passed_on, part, part_got, whole,
     load_sem, halo_send, halo_recv, z_send, z_recv, grad_send, grad_recv,
 ):
@@ -128,8 +128,7 @@
     rel_copies = spread_copies(2, 2 * steps + 3, rel_src, rel_turned, rel_right)
     cor_copies = spread_copies(4, 2 * steps + 4, cor_src, cor_turned, cor_right)
     z_g = to_previous(6, g_src, g_got)
-    z_rel_p0 = to_previous(7, adj.at[0], rel_p0)
-    z_cor_p0 = to_previous(8, cor.at[0], cor_p0)
+    z_change = to_previous(7, change, change_got)
 
     rel_right[...] = jnp.zeros_like(rel_right)
     cor_right[...] = jnp.zeros_like(cor_right)
@@ -347,10 +346,6 @@
                     rel_turned[i, thick - 1 - p] = value
             spread_start(rel_copies)
 
-            @pl.when(jnp.logical_and(has_prev, has_next))
-            def _():
-                z_rel_p0.start()
-
     def send_corrected():
         for i in range(MASSIVE):
             for p in range(thick):
@@ -358,6 +353,9 @@
                 cor_src[i, p] = value
                 cor_turned[i, thick - 1 - p] = value
         spread_start(cor_copies)
+        for i in range(FIELDS):
+            change[i] = cor[0, i] - adj[0, i]
+        pl.when(has_prev)(z_change.start)
 
     @pl.when(t == tms - 1)
     def _():
@@ -366,11 +364,6 @@
             cor[0, i] = zero_q[i] + (adj[0, i] - zero_q[i])
             cor[1, i] = zero_p1 + (adj[1, i] - zero_p1)
         send_corrected()
-
-        @pl.when(has_prev)
-        def _():
-            z_rel_p0.start()
-            z_cor_p0.start()
 
     for n in range(last, -1, -1):
         for i in range(FIELDS):
@@ -420,10 +413,9 @@
             pl.when(has_other)(rel_copies[1].wait_recv)
 
         solve(rel_right, inv.at[coarse], rel_q, rel_copies[2].wait_recv, far)
-        z_rel_p0.wait_recv()
         for i in range(FIELDS):
             offs[0, i] = adj[0, i] - rel_q[i]
-            offs[1, i] = adj[1, i] - 0.5 * (rel_q[i] + rel_p0[i])
+            offs[1, i] = adj[1, i] - 0.5 * rel_q[i]
 
     def share_gradient():
         for copy in grad_one:
@@ -447,12 +439,11 @@
             pl.when(has_other)(cor_copies[1].wait_recv)
 
         solve(cor_right, inv.at[coarse], cor_q, cor_copies[2].wait_recv, far)
-        z_cor_p0.wait_recv()
+        z_change.wait_recv()
         for i in range(FIELDS):
             cor[0, i] = cor_q[i] + offs[0, i]
-            cor[1, i] = 0.5 * (cor_q[i] + cor_p0[i]) + offs[1, i]
+            cor[1, i] = 0.5 * (cor_q[i] + change_got[i]) + offs[1, i]
         send_corrected()
-        pl.when(has_prev)(z_cor_p0.start)
 
     pl.when(t == tms - 2)(share_gradient)
 
@@ -485,7 +476,7 @@
         for copies in (w_copies, rel_copies, cor_copies):
             copies[0].wait_send()
             pl.when(has_other)(copies[1].wait_send)
-        for copy in (z_g, z_rel_p0, z_cor_p0):
+        for copy in (z_g, z_change):
             copy.wait_send()
 
     for copy in grad_one + grad_two:
@@ -533,9 +524,9 @@
             heavy,
             heavy,
             heavy,
+            heavy,
+            heavy,
             every,
-            heavy,
-            heavy,
             every,
             vmem(3, MASSIVE, thick),
             vmem(FIELDS * thick),
@@ -544,8 +535,8 @@
             pltpu.SemaphoreType.DMA((4,)),
             pltpu.SemaphoreType.DMA((2 * steps + 5, 2)),
             pltpu.SemaphoreType.DMA((2 * steps + 5, 2)),
-            pltpu.SemaphoreType.DMA((9,)),
-            pltpu.SemaphoreType.DMA((9,)),
+            pltpu.SemaphoreType.DMA((8,)),
+            pltpu.SemaphoreType.DMA((8,)),
             pltpu.SemaphoreType.DMA((2, tms - 1)),
             pltpu.SemaphoreType.DMA((2, tms - 1)),
         ],

time: 43.8 us -> 42.8 us (0.977)
  Pallas kernels: 40.8 us -> 39.7 us
    pallas_call x1, Pallas kernels: 40.8 us -> 39.7 us  [on_device(): pl.pallas_call(functools.partial(kernel, steps, thick, tms, spaces), out_...]
where the time goes in v4:
time: 42.8 us; the launch traced here: 42.6 us
  Pallas kernels  39.7 us (93%)
  local copies, waits for them, and re-layouts  2.23 us (5%)
  between operations  0.65 us (2%)
    pallas_call x1, Pallas kernels, on_device(): pl.pallas_call(functools.partial(kernel, steps, thick, tms, spaces), out_...  39.7 us
    unnamed x4, local copies, waits for them, and re-layouts  2.23 us

profile of v4, /device:TPU:3, one launch (start us, length us, event | category | flops | bytes accessed | tf_op | source)
XLA Modules:
  0.0 42.6 jit_solution(1452331099516327926)
XLA Ops:
  0.6 39.7 %adjoint_cycle.1 = (f32[1,2,4,4,8,128]{5,4,3,2,1,0:T(8,128)}, f32[4,4,8,128]{3,2,1,0:T(8,128)}) custom-call(bf16[4,4,4,8,128]{4,3,2,1,0:T(8,128)(2,1)} %states_hbm.1, f32[4,4,4,8,128]{4,3,2,1,0:T(8,128)} %source_hbm.1, f32[4,4,8,128]{3,2,1,0:T(8,128)} %gain_hbm.1, f32[1,2,4,4,8,128]{5,4,3,2,1,0:T(8,128)} %guess_hbm.1), custom_call_target="tpu_custom_call" | custom-call | tf_op jit(solution)/shard_map/adjoint_cycle/pallas_call | solution.py:494
  40.4 0.0 copy-start
  40.4 1.6 %copy.8 = f32[1,2,4,4,8,128]{5,4,3,2,1,0:T(8,128)} copy(f32[1,2,4,4,8,128]{5,4,3,2,1,0:T(8,128)} %get-tuple-element.4) | data formatting | bytes 262144
  42.0 0.0 copy-done
  42.0 0.6 %copy.9 = f32[4,4,8,128]{3,2,1,0:T(8,128)} copy(f32[4,4,8,128]{3,2,1,0:T(8,128)S(1)} %copy-done) | data formatting | bytes 131072
Async XLA Ops:
  40.4 1.6 %copy-start = (f32[4,4,8,128]{3,2,1,0:T(8,128)S(1)}, f32[4,4,8,128]{3,2,1,0:T(8,128)}, u32[]{:S(2)}) copy-start(f32[4,4,8,128]{3,2,1,0:T(8,128)} %get-tuple-element.5) | copy-start | bytes 196612

commit v5 on v4

--- a/solution.py
+++ b/solution.py
@@ -423,7 +423,7 @@
         total = part[pl.ds(t * chunk, chunk)]
         for hop in range(1, tms):
             total = total + part_got[hop - 1]
-        whole[pl.ds(t * chunk, chunk)] = time_step * total
+        whole[pl.ds(t * chunk, chunk)] = total
         for copy in grad_two:
             copy.start()
 
@@ -491,7 +491,7 @@
     in_vmem = pl.BlockSpec(memory_space=pltpu.VMEM)
     heavy = vmem(MASSIVE, thick)
     every = vmem(FIELDS, thick)
-    return pl.pallas_call(
+    corrected, summed = pl.pallas_call(
         functools.partial(kernel, steps, thick, tms, spaces),
         out_shape=(
             jax.ShapeDtypeStruct(guess_pairs.shape, jnp.float32),
@@ -545,6 +545,7 @@
         ),
         name="adjoint_cycle",
     )(forward_states, adjoint_source, source_gain, guess_pairs)
+    return corrected, time_step * summed
 
 
 def solution(mesh):

time: 42.8 us -> 42.7 us (level)
  local copies, waits for them, and re-layouts: 2.23 us -> 0.66 us
  other arithmetic: 0 us -> 1.51 us
    unnamed x4 -> x3, local copies, waits for them, and re-layouts: 2.23 us -> 0.66 us
    mul x0 -> x1, other arithmetic: none -> 1.51 us  [on_device(): return (corrected, time_step * summed)]
where the time goes in v5:
time: 42.7 us; the launch traced here: 42.5 us
  Pallas kernels  39.7 us (93%)
  other arithmetic  1.51 us (4%)
  local copies, waits for them, and re-layouts  0.66 us (2%)
  between operations  0.65 us (2%)
    pallas_call x1, Pallas kernels, on_device(): pl.pallas_call(functools.partial(kernel, steps, thick, tms, spaces), out_...  39.7 us
    mul x1, other arithmetic, on_device(): return (corrected, time_step * summed)  1.51 us

profile of v5, /device:TPU:3, one launch (start us, length us, event | category | flops | bytes accessed | tf_op | source)
XLA Modules:
  0.0 42.5 jit_solution(13029363278035289042)
XLA Ops:
  0.6 39.7 %adjoint_cycle.1 = (f32[1,2,4,4,8,128]{5,4,3,2,1,0:T(8,128)}, f32[4,4,8,128]{3,2,1,0:T(8,128)}) custom-call(bf16[4,4,4,8,128]{4,3,2,1,0:T(8,128)(2,1)} %states_hbm.1, f32[4,4,4,8,128]{4,3,2,1,0:T(8,128)} %source_hbm.1, f32[4,4,8,128]{3,2,1,0:T(8,128)} %gain_hbm.1, f32[1,2,4,4,8,128]{5,4,3,2,1,0:T(8,128)} %guess_hbm.1), custom_call_target="tpu_custom_call" | custom-call | tf_op jit(solution)/shard_map/adjoint_cycle/pallas_call | solution.py:494
  40.4 0.0 copy-start
  40.4 1.5 %broadcast_multiply_fusion = f32[4,4,8,128]{3,2,1,0:T(8,128)} fusion(f32[4,4,8,128]{3,2,1,0:T(8,128)} %get-tuple-element.5), kind=kLoop, calls=%fused_computation | loop fusion | flops 16384 | bytes 131072 | tf_op jit(solution)/shard_map/mul | solution.py:548
  41.9 0.0 copy-done
  41.9 0.7 %copy.7 = f32[1,2,4,4,8,128]{5,4,3,2,1,0:T(8,128)} copy(f32[1,2,4,4,8,128]{5,4,3,2,1,0:T(8,128)S(1)} %copy-done) | data formatting | bytes 262144
Async XLA Ops:
  40.4 1.5 %copy-start = (f32[1,2,4,4,8,128]{5,4,3,2,1,0:T(8,128)S(1)}, f32[1,2,4,4,8,128]{5,4,3,2,1,0:T(8,128)}, u32[]{:S(2)}) copy-start(f32[1,2,4,4,8,128]{5,4,3,2,1,0:T(8,128)} %get-tuple-element.8) | copy-start | bytes 393220
